TPU v7x, 256 devices: a whole 4x4x8 slice. The times are simulated.
256 devices in a mesh: input: 8 (over y_hi, x), freq: 16 (over z, core), tm: 2 (over y_lo).
Axes of the slice: x: 4, y: 4 (y_hi: 2, y_lo: 2; y = y_hi * 2 + y_lo), z: 8, core: 2. Of those that a mesh axis runs over, the one named last changes fastest.
Arguments:
- voltages: bfloat16 [1024, 256, 2048], P(('input', 'freq'), 'tm'), may hold values from -6 to 6
- taps: float32 [4, 2048], replicated, may hold values from -0.09375 to 0.09375
Outputs:
- visibilities: bfloat16 [2, 512, 1024, 1024], P(None, ('input', 'freq'), 'tm')
All inputs are finite; a program needn't handle non-finite values.
Results may differ from a plain program's by a relative error of at most 0.012.
Values may be sent and summed in bfloat16 or wider, within the bound.
No kernel may reach another device: no remote copies, remote signals or barrier semaphores. Data moves between devices by JAX's collectives and lax.ppermute only.
A program may use at most 128 MiB of HBM per device.

v0:
```python
import math

import jax
import jax.numpy as jnp
from jax import lax
from jax.sharding import PartitionSpec as P

CH = 512


def passed_along(block, axis, distance):
    devices = range(lax.axis_size(axis))
    route = [(i - distance, i) for i in devices if i - distance in devices]
    return lax.ppermute(block, axis, route)


def dft_table(npoints):
    chan = lax.broadcasted_iota(jnp.int32, (CH, npoints), 0)
    sample = lax.broadcasted_iota(jnp.int32, (CH, npoints), 1)
    phase = chan * sample % npoints
    angle = phase.astype(jnp.float32) * (2.0 * math.pi / npoints)
    return jnp.stack([jnp.cos(angle), -jnp.sin(angle)]).astype(jnp.bfloat16)


def swap_parts(block, count):
    parts = block.reshape(block.shape[0], block.shape[1], -1, 2, count)
    swapped = jnp.stack([parts[:, :, :, 1], -parts[:, :, :, 0]], axis=3)
    return swapped.reshape(block.shape)


def pair_products(left, right, count):
    left_swap = swap_parts(left, count)
    real = jnp.einsum("nik,njk->nij", left, right, preferred_element_type=jnp.float32)
    imag = jnp.einsum("nik,njk->nij", left_swap, right, preferred_element_type=jnp.float32)
    return jnp.stack([real, imag])


def body(voltages, taps):
    ntaps = taps.shape[0]
    count = voltages.shape[1]
    npoints = voltages.shape[2]
    width_in = voltages.shape[0]
    ntime = lax.axis_size("tm")
    scale = 1.0 / (count * ntime)
    history = passed_along(voltages[:, count - (ntaps - 1) :, :], "tm", 1)
    framed = jnp.concatenate([history, voltages], axis=1).astype(jnp.float32)
    total = jnp.zeros((width_in, count, npoints), jnp.float32)
    for lag in range(ntaps):
        total = total + taps[lag] * framed[:, ntaps - 1 - lag : ntaps - 1 - lag + count]
    filtered = total.astype(jnp.bfloat16)
    table = dft_table(npoints)
    spectra = jnp.einsum(
        "rcs,its->cirt", table, filtered, preferred_element_type=jnp.float32
    ).astype(jnp.bfloat16)
    groups = lax.axis_size("input") * lax.axis_size("freq")
    per_group = CH // groups
    spectra = spectra.reshape(groups, per_group, 1, 1, width_in * 2 * count)
    block = lax.all_to_all(spectra, ("input", "freq"), split_axis=0, concat_axis=2, tiled=True)
    items = block.shape[1]
    local = block.reshape(items, -1, 2 * count)
    full = lax.all_gather(local, "tm", axis=2, tiled=True)
    rows = full.shape[1] // ntime
    start = lax.axis_index("tm") * rows
    left = lax.dynamic_slice_in_dim(full, start, rows, 1)
    stacked = pair_products(left, full, count)
    return (stacked * scale).astype(jnp.bfloat16)


def solution(mesh):
    in_specs = (P(("input", "freq"), "tm", None), P())
    out_specs = P(None, ("input", "freq"), "tm", None)
    return jax.shard_map(body, mesh=mesh, in_specs=in_specs, out_specs=out_specs, check_vma=False)
```

profile of v0, /device:TPU:38, one launch (start us, length us, event | category | flops | bytes accessed | tf_op | source)
XLA Modules:
  0.0 221.1 jit_solution(2078045148092382161)
XLA Ops:
  6.5 0.0 copy-start.3
  6.5 0.0 all-gather.2.cloned.1.call-start
  6.5 0.0 copy-start
  6.5 1.2 slice.34
  7.7 3.6 %collective-permute-start = (bf16[8,3,2048]{2,1,0:T(4,128)(2,1)S(1)}, bf16[8,3,2048]{2,1,0:T(4,128)(2,1)S(1)}, u32[]{:S(2)}, u32[]{:S(2)}) collective-permute-start(bf16[8,3,2048]{2,1,0:T(4,128)(2,1)S(1)} %slice.34), channel_id=1, source_target_pairs={{0,1},{2,3},{4,5},{6,7},{8,9},{10,11},{12,13},{14,15},{16,17},{18,... | collective-permute-start | bytes 294920 | tf_op jit(solution)/shard_map/ppermute | solution.py:14
  11.3 17.6 %negate_convert_fusion = (bf16[1,512,2048]{2,1,0:T(8,128)(2,1)S(1)}, bf16[1,512,2048]{2,1,0:T(8,128)(2,1)}) fusion(), kind=kLoop, calls=%fused_computation.22 | loop fusion | flops 17825792 | bytes 4194304 | tf_op jit(solution)/shard_map/convert.1
  29.0 0.0 copy-done.3
  29.0 0.0 collective-permute-done
  29.0 0.0 copy-done
  29.0 4.8 %maximum_convert_fusion = f32[8,131,2048]{2,1,0:T(8,128)} fusion(bf16[8,128,2048]{2,1,0:T(8,128)(2,1)S(1)} %copy-done, bf16[8,3,2048]{2,1,0:T(4,128)(2,1)S(1)} %collective-permute-done), kind=kLoop, calls=%fused_computation.13 | loop fusion | flops 8585216 | bytes 12877824 | tf_op jit(solution)/shard_map/convert_element_type | solution.py:46
  33.8 16.4 %convert_bitcast_fusion = bf16[512,8,2,128]{0,3,2,1:T(8,128)(2,1)} fusion(bf16[1,512,2048]{2,1,0:T(8,128)(2,1)S(1)} %get-tuple-element.11, bf16[1,512,2048]{2,1,0:T(8,128)(2,1)} %get-tuple-element.12, f32[8,131,2048]{2,1,0:T(8,128)} %maximum_convert_fusion, f32[2048]{0:T(1024)S(1)} %bitcast.38, f32[2048]{0:T(1024)S(1)} %bitcast.39, f32[2048]{0:T(1024)S(1)} %bitcast.37, ...), kind=kOutput, calls=%fused_computation.34 | convolution fusion | flops 4321181696 | bytes 39878656 | tf_op jit(solution)/shard_map/rcs,its->cirt/dot_general | solution.py:52
  50.2 4.9 %copy.6 = bf16[512,8,2,128]{3,2,1,0:T(2,128)(2,1)S(1)} copy(bf16[512,8,2,128]{0,3,2,1:T(8,128)(2,1)} %convert_bitcast_fusion) | data formatting | bytes 4194304 | tf_op jit(solution)/shard_map/convert_element_type | solution.py:54
  55.1 2.0 reshape.78
  57.1 64.7 %all_to_all.15 = bf16[128,4,1,1,2048]{4,1,3,2,0:T(4,128)(2,1)S(1)} all-to-all(bf16[128,4,1,1,2048]{4,1,3,2,0:T(4,128)(2,1)} %bitcast.34), channel_id=1, replica_groups=mesh['input'=8,'freq'=16,'tm'=2] {'input','freq'}, dimensions={0} | all-to-all | bytes 4194304 | tf_op jit(solution)/shard_map/all_to_all | solution.py:58
  121.8 1.2 copy.8
  123.0 2.3 %reshape.79 = bf16[4,1024,256]{2,1,0:T(8,128)(2,1)} reshape(bf16[1,4,128,1,1,2048]{5,2,1,4,3,0:T(8,128)(2,1)S(1)} %copy.8) | data formatting | bytes 4194304 | tf_op jit(solution)/shard_map/reshape | solution.py:60
  125.3 0.0 all-gather.2.cloned.1.call-update
  125.4 60.0 %all-gather.2.cloned.1.call-done = bf16[4,1024,512]{2,1,0:T(8,128)(2,1)} async-done(((bf16[4,1024,256]{2,1,0:T(8,128)(2,1)}), bf16[4,1024,512]{2,1,0:T(8,128)(2,1)}) %all-gather.2.cloned.1.call-update) | async-done | bytes 4194320 | tf_op jit(solution)/shard_map/all_gather | solution.py:61
  185.4 3.0 %constant_dynamic-slice_fusion = bf16[4,512,512]{2,1,0:T(8,128)(2,1)} fusion(bf16[4,1024,512]{2,1,0:T(8,128)(2,1)} %all-gather.2.cloned.1.call-done, s32[]{:T(128)S(6)} %select_n.24), kind=kLoop, calls=%fused_computation.35 | loop fusion | bytes 4194308 | tf_op jit(solution)/shard_map/dynamic_slice | solution.py:64
  188.4 2.5 %reshape.80 = bf16[4,512,2,2,128]{4,3,2,1,0:T(2,128)(2,1)S(1)} reshape(bf16[4,512,512]{2,1,0:T(8,128)(2,1)} %constant_dynamic-slice_fusion) | data formatting | bytes 4194304 | tf_op jit(solution)/shard_map/reshape | solution.py:26
  191.0 3.9 %fusion.22 = (bf16[4,512,2,1,128]{4,3,2,1,0:T(2,128)(2,1)S(1)}, bf16[4,512,2,1,128]{4,3,2,1,0:T(2,128)(2,1)S(1)}) fusion(bf16[4,512,2,2,128]{4,3,2,1,0:T(2,128)(2,1)S(1)} %reshape.80), kind=kLoop, calls=%fused_computation.37 | loop fusion | flops 524288 | bytes 4194304 | tf_op jit(solution)/shard_map/slice | solution.py:27
  194.8 4.8 %pad_maximum_fusion = bf16[4,512,2,2,128]{4,3,2,1,0:T(2,128)(2,1)S(1)} fusion(bf16[4,512,2,1,128]{4,3,2,1,0:T(2,128)(2,1)S(1)} %get-tuple-element.6, bf16[4,512,2,1,128]{4,3,2,1,0:T(2,128)(2,1)S(1)} %get-tuple-element.5), kind=kLoop, calls=%fused_computation.33 | loop fusion | flops 4194304 | bytes 4194304 | tf_op jit(solution)/shard_map/stack | solution.py:27
  199.7 2.2 %reshape.81 = bf16[4,512,512]{2,1,0:T(8,128)(2,1)} reshape(bf16[4,512,2,2,128]{4,3,2,1,0:T(2,128)(2,1)S(1)} %pad_maximum_fusion) | data formatting | bytes 4194304 | tf_op jit(solution)/shard_map/reshape | solution.py:28
  201.9 0.0 copy-start.1
  201.9 0.0 copy-start.2
  201.9 5.3 %convolution_bitcast_fusion.1 = f32[1,4,512,1024]{3,2,1,0:T(8,128)S(1)} fusion(bf16[4,512,512]{2,1,0:T(8,128)(2,1)} %constant_dynamic-slice_fusion, bf16[4,1024,512]{2,1,0:T(8,128)(2,1)} %all-gather.2.cloned.1.call-done), kind=kOutput, calls=%fused_computation.31 | convolution fusion | flops 2147483648 | bytes 14680064 | tf_op jit(solution)/shard_map/nik,njk->nij/dot_general | solution.py:33
  207.3 0.0 copy-done.1
  207.3 0.0 copy-done.2
  207.3 2.4 %convolution_bitcast_fusion = f32[1,4,512,1024]{3,2,1,0:T(8,128)S(1)} fusion(bf16[4,512,512]{2,1,0:T(8,128)(2,1)S(1)} %copy-done.1, bf16[4,1024,512]{2,1,0:T(8,128)(2,1)S(1)} %copy-done.2), kind=kOutput, calls=%fused_computation.30 | convolution fusion | flops 2147483648 | bytes 14680064 | tf_op jit(solution)/shard_map/nik,njk->nij/dot_general | solution.py:34
  209.7 4.6 %fusion = bf16[2,4,512,1024]{3,2,1,0:T(8,128)(2,1)} fusion(f32[1,4,512,1024]{3,2,1,0:T(8,128)S(1)} %convolution_bitcast_fusion, f32[1,4,512,1024]{3,2,1,0:T(8,128)S(1)} %convolution_bitcast_fusion.1), kind=kLoop, calls=%fused_computation.1 | loop fusion | flops 12582912 | bytes 25165824 | tf_op jit(solution)/shard_map/convert_element_type | solution.py:66
  (1 shorter events, 0.0 us)
Async XLA Ops:
  6.5 22.4 %copy-start.3 = (f32[4,2048]{1,0:T(4,128)S(1)}, f32[4,2048]{1,0:T(4,128)}, u32[]{:S(2)}) copy-start(f32[4,2048]{1,0:T(4,128)} %param.3) | copy-start | bytes 98308
  6.5 178.9 %all-gather.2.cloned.1.call-start = ((), (), s32[]{:S(2)}) async-start(), calls=%async_computation.1 | async-start | bytes 6291456 | tf_op jit(solution)/shard_map/all_gather | solution.py:61
  6.5 22.5 %copy-start = (bf16[8,128,2048]{2,1,0:T(8,128)(2,1)S(1)}, bf16[8,128,2048]{2,1,0:T(8,128)(2,1)}, u32[]{:S(2)}) copy-start(bf16[8,128,2048]{2,1,0:T(8,128)(2,1)} %param.2) | copy-start | bytes 12582916
  7.7 21.3 %collective-permute-start = (bf16[8,3,2048]{2,1,0:T(4,128)(2,1)S(1)}, bf16[8,3,2048]{2,1,0:T(4,128)(2,1)S(1)}, u32[]{:S(2)}, u32[]{:S(2)}) collective-permute-start(bf16[8,3,2048]{2,1,0:T(4,128)(2,1)S(1)} %slice.34), channel_id=1, source_target_pairs={{0,1},{2,3},{4,5},{6,7},{8,9},{10,11},{12,13},{14,15},{16,17},{18,... | collective-permute-start | bytes 294920 | tf_op jit(solution)/shard_map/ppermute | solution.py:14
  201.9 5.3 %copy-start.1 = (bf16[4,512,512]{2,1,0:T(8,128)(2,1)S(1)}, bf16[4,512,512]{2,1,0:T(8,128)(2,1)}, u32[]{:S(2)}) copy-start(bf16[4,512,512]{2,1,0:T(8,128)(2,1)} %reshape.81) | copy-start | bytes 6291460
  201.9 5.4 %copy-start.2 = (bf16[4,1024,512]{2,1,0:T(8,128)(2,1)S(1)}, bf16[4,1024,512]{2,1,0:T(8,128)(2,1)}, u32[]{:S(2)}) copy-start(bf16[4,1024,512]{2,1,0:T(8,128)(2,1)} %all-gather.2.cloned.1.call-done) | copy-start | bytes 12582916
Sparse Core Ops, SparseCore 0:
  125.5 59.8 all-gather.1
where the time goes:
time: 223 us; the launch traced here: 221 us
  blocking collectives  64.7 us (29%)
  waiting for transfers between devices  60 us (27%)
  other arithmetic  35.6 us (16%)
  matrix products  24.1 us (11%)
  local copies, waits for them, and re-layouts  19.5 us (9%)
  between operations  13.5 us (6%)
  starting transfers between devices  3.62 us (2%)
    all_to_all x1, blocking collectives, body(): lax.all_to_all(spectra, ('input', 'freq'), split_axis=0, concat_axis=2, t...  64.7 us
    all_gather x1, waiting for transfers between devices, body(): full = lax.all_gather(local, 'tm', axis=2, tiled=True)  60 us
    another operation x1, other arithmetic  17.6 us
    dot_general x1, matrix products, body(): jnp.einsum('rcs,its->cirt', table, filtered, preferred_element_type=jnp.f...  16.4 us
    dot_general x1, matrix products, pair_products(): jnp.einsum('nik,njk->nij', left, right, preferred_element_type=jnp.float32)  5.34 us
    convert_element_type x1, local copies, waits for them, and re-layouts, body(): spectra = jnp.einsum('rcs,its->cirt', table, filtered, preferred_element_...  4.94 us
    another operation x1, other arithmetic, swap_parts(): swapped = jnp.stack([parts[:, :, :, 1], -parts[:, :, :, 0]], axis=3)  4.84 us
    convert_element_type x1, other arithmetic, body(): framed = jnp.concatenate([history, voltages], axis=1).astype(jnp.float32)  4.77 us
  transfers between devices with their start and end apart: 2, of which 1 were waited for; matrix products, arithmetic and copies ran while one was open for 8% of the time, Pallas kernels for 0%

commit v1 on v0

v1 whole, which is shorter than its diff:
```python
import functools
import math

import jax
import jax.numpy as jnp
from jax import lax
from jax.experimental import pallas as pl
from jax.experimental.pallas import tpu as pltpu
from jax.sharding import PartitionSpec as P

CH = 512
LANES = 128
MIB = 1024 * 1024


def passed_along(block, axis, distance):
    devices = range(lax.axis_size(axis))
    route = [(i - distance, i) for i in devices if i - distance in devices]
    return lax.ppermute(block, axis, route)


def swapped(block, axis):
    size = lax.axis_size(axis)
    return lax.ppermute(block, axis, [(i, size - 1 - i) for i in range(size)])


def tables(npoints, groups, per_group):
    half, quarter = npoints // 2, npoints // 4
    unit = 2.0 * math.pi / npoints
    group = lax.broadcasted_iota(jnp.int32, (groups, quarter), 0)
    sample = lax.broadcasted_iota(jnp.int32, (groups, quarter), 1)
    angle = ((per_group * group * sample) % npoints).astype(jnp.float32) * unit
    cos_base, sin_base = jnp.cos(angle), jnp.sin(angle)
    cos_base, sin_base = lax.optimization_barrier((cos_base, sin_base))
    out = [jnp.concatenate([cos_base, -sin_base]).astype(jnp.bfloat16)]
    for j in range(1, per_group):
        depth = quarter if j % 2 == 0 else half
        turn = ((j * jnp.arange(depth, dtype=jnp.int32)) % npoints).astype(jnp.float32) * unit
        cos_turn, sin_turn = jnp.cos(turn), jnp.sin(turn)
        cos_wide = jnp.tile(cos_base, (1, depth // quarter))
        sin_wide = jnp.tile(sin_base, (1, depth // quarter))
        real = cos_wide * cos_turn - sin_wide * sin_turn
        imag = -(sin_wide * cos_turn + cos_wide * sin_turn)
        out.append(jnp.concatenate([real, imag]).astype(jnp.bfloat16))
    return out


def filter_kernel(volt_ref, hist_ref, taps_ref, sum_ref, alt_ref, diff_ref):
    ntaps = taps_ref.shape[0]
    count = volt_ref.shape[1]
    quarter = sum_ref.shape[1]
    nhist = hist_ref.shape[1]
    pad = 8

    def filtered(start):
        lanes = slice(start, start + LANES)
        hist = hist_ref[0, :, lanes].astype(jnp.float32)
        body = volt_ref[0, :, lanes].astype(jnp.float32)
        top = jnp.zeros((pad - nhist, LANES), jnp.float32)
        wide = jnp.concatenate([top, hist, body], axis=0)
        total = taps_ref[ntaps - 1, lanes] * wide
        for lag in range(ntaps - 2, -1, -1):
            total = pltpu.roll(total, 1, 0) + taps_ref[lag, lanes] * wide
        return total[pad:]

    for start in range(0, quarter, LANES):
        here = slice(start, start + LANES)
        first, third = filtered(start), filtered(start + 2 * quarter)
        diff_ref[:, here] = (first - third).astype(jnp.bfloat16)
        even = first + third
        second, fourth = filtered(start + quarter), filtered(start + 3 * quarter)
        there = slice(start + quarter, start + quarter + LANES)
        diff_ref[:, there] = (second - fourth).astype(jnp.bfloat16)
        odd = second + fourth
        sum_ref[:, here] = (even + odd).astype(jnp.bfloat16)
        alt_ref[:, here] = (even - odd).astype(jnp.bfloat16)


def filter_bank(voltages, history, taps):
    width, count, npoints = voltages.shape
    half, quarter = npoints // 2, npoints // 4
    rows = width * count
    depths = (quarter, quarter, half)
    return pl.pallas_call(
        filter_kernel,
        grid=(width,),
        in_specs=[
            pl.BlockSpec((1, count, npoints), lambda i: (i, 0, 0)),
            pl.BlockSpec((1, history.shape[1], npoints), lambda i: (i, 0, 0)),
            pl.BlockSpec(taps.shape, lambda i: (0, 0)),
        ],
        out_specs=[pl.BlockSpec((count, d), lambda i: (i, 0)) for d in depths],
        out_shape=[jax.ShapeDtypeStruct((rows, d), jnp.bfloat16) for d in depths],
        compiler_params=pltpu.CompilerParams(vmem_limit_bytes=48 * MIB),
        cost_estimate=pl.CostEstimate(flops=20 * rows * npoints, bytes_accessed=4 * rows * npoints, transcendentals=0),
        name="filter_bank",
    )(voltages, history, taps)


def spectra_kernel(width, table_ref, filt_ref, out_ref, wide_ref):
    rows = filt_ref.shape[0]
    count = rows // width
    groups = out_ref.shape[0]
    pair = 2 * count
    for step in range(rows // pair):
        product = lax.dot_general(
            table_ref[...], filt_ref[step * pair : (step + 1) * pair, :],
            (((1,), (1,)), ((), ())), preferred_element_type=jnp.float32,
        )
        wide_ref[2 * step] = product[:, :count]
        wide_ref[2 * step + 1] = product[:, count:]

    for g in range(groups):
        real = wide_ref[:, g, :]
        imag = wide_ref[:, groups + g, :]
        out_ref[g] = jnp.concatenate([real, imag], axis=0).astype(jnp.bfloat16)


def spectra(table, filt, width, groups):
    rows, depth = filt.shape
    count = rows // width
    return pl.pallas_call(
        functools.partial(spectra_kernel, width),
        out_shape=jax.ShapeDtypeStruct((groups, 2 * width, count), jnp.bfloat16),
        in_specs=[pl.BlockSpec(memory_space=pltpu.VMEM)] * 2,
        out_specs=pl.BlockSpec(memory_space=pltpu.VMEM),
        scratch_shapes=[pltpu.VMEM((width, 2 * groups, count), jnp.float32)],
        compiler_params=pltpu.CompilerParams(vmem_limit_bytes=48 * MIB),
        cost_estimate=pl.CostEstimate(
            flops=4 * groups * rows * depth, bytes_accessed=2 * rows * depth, transcendentals=0
        ),
        name="spectra",
    )(table, filt)


def correlate_kernel(width, scale, first, *refs):
    if first:
        tm_ref, own_ref, other_ref, out_ref, real_ref, imag_ref = refs
    else:
        tm_ref, own_ref, other_ref, _, out_ref, real_ref, imag_ref = refs
    groups, _, count = own_ref.shape
    inputs = groups * width
    rows = out_ref.shape[2]
    for at, ref in enumerate((own_ref, other_ref)):
        wide = ref[...].astype(jnp.float32).reshape(groups, 2, width, count)
        real = wide[:, 0].reshape(inputs, count).astype(jnp.bfloat16)
        imag = wide[:, 1].reshape(inputs, count).astype(jnp.bfloat16)
        lanes = slice(at * count, (at + 1) * count)
        real_ref[:, lanes] = real
        imag_ref[:, lanes] = imag
    start = pl.multiple_of(tm_ref[0] * rows, rows)
    contract = (((1,), (1,)), ((), ()))
    dot = functools.partial(lax.dot_general, dimension_numbers=contract, preferred_element_type=jnp.float32)
    step = min(256, rows)
    for at in range(0, rows, step):
        a = real_ref[pl.ds(pl.multiple_of(start + at, step), step), :]
        b = imag_ref[pl.ds(pl.multiple_of(start + at, step), step), :]
        u = real_ref[...]
        w = imag_ref[...]
        out_ref[0, 0, at : at + step] = ((dot(a, u) + dot(b, w)) * scale).astype(jnp.bfloat16)
        out_ref[1, 0, at : at + step] = ((dot(b, u) - dot(a, w)) * scale).astype(jnp.bfloat16)


def correlate(tm, own, other, result, channel, channels, width, parts):
    groups, _, count = own.shape
    inputs = groups * width
    rows = inputs // parts
    scale = 1.0 / (parts * count)
    whole = pl.BlockSpec(own.shape, lambda i: (0, 0, 0))
    args = [tm, own, other]
    in_specs = [pl.BlockSpec(memory_space=pltpu.SMEM), whole, whole]
    aliases = {}
    if result is not None:
        args.append(result)
        in_specs.append(pl.BlockSpec(memory_space=pl.ANY))
        aliases = {3: 0}
    return pl.pallas_call(
        functools.partial(correlate_kernel, width, scale, result is None),
        grid=(1,),
        in_specs=in_specs,
        out_specs=pl.BlockSpec((2, 1, rows, inputs), lambda i: (0, channel, 0, 0)),
        out_shape=jax.ShapeDtypeStruct((2, channels, rows, inputs), jnp.bfloat16),
        scratch_shapes=[pltpu.VMEM((inputs, parts * count), jnp.bfloat16)] * 2,
        input_output_aliases=aliases,
        compiler_params=pltpu.CompilerParams(vmem_limit_bytes=48 * MIB),
        cost_estimate=pl.CostEstimate(
            flops=8 * rows * inputs * parts * count, bytes_accessed=4 * rows * inputs, transcendentals=0
        ),
        name="correlate",
    )(*args)


def after_kernel(*refs):
    pass


def after(block, *earlier):
    return pl.pallas_call(
        after_kernel,
        out_shape=jax.ShapeDtypeStruct(block.shape, block.dtype),
        in_specs=[pl.BlockSpec(memory_space=pl.ANY)] * (1 + len(earlier)),
        out_specs=pl.BlockSpec(memory_space=pl.ANY),
        input_output_aliases={0: 0},
        cost_estimate=pl.CostEstimate(flops=0, bytes_accessed=0, transcendentals=0),
        name="after",
    )(block, *earlier)


def body(voltages, taps):
    width, count, npoints = voltages.shape
    parts = lax.axis_size("tm")
    groups = lax.axis_size("input") * lax.axis_size("freq")
    per_group = CH // groups
    history = passed_along(voltages[:, count - 4 :, :], "tm", 1)
    table = tables(npoints, groups, per_group)
    sums, alts, diffs = filter_bank(voltages, history, taps)
    sources = [sums, diffs, alts, diffs]
    tm = lax.axis_index("tm").astype(jnp.int32).reshape(1)
    own, other = [], []
    for j in range(per_group):
        block = spectra(table[j], sources[j], width, groups)
        if j >= 2:
            block = after(block, other[j - 2])
        block = lax.all_to_all(block, ("input", "freq"), split_axis=0, concat_axis=0, tiled=True)
        own.append(block)
        other.append(swapped(block, "tm"))
    result = None
    for j in range(per_group):
        result = correlate(tm, own[j], other[j], result, j, per_group, width, parts)
    return result


def solution(mesh):
    in_specs = (P(("input", "freq"), "tm", None), P())
    out_specs = P(None, ("input", "freq"), "tm", None)
    return jax.shard_map(body, mesh=mesh, in_specs=in_specs, out_specs=out_specs, check_vma=False)
```

time: 223 us -> 166 us (0.74)
  blocking collectives: 64.7 us -> 0 us
  starting transfers between devices: 3.62 us -> 59.2 us
  other arithmetic: 35.6 us -> 5 us
  Pallas kernels: 0 us -> 26.4 us
  matrix products: 24.1 us -> 0 us
  between operations: 13.5 us -> 0.19 us
  local copies, waits for them, and re-layouts: 19.5 us -> 8.76 us
  waiting for transfers between devices: 60 us -> 63.6 us
    all_to_all x1 -> x0, blocking collectives: 64.7 us -> none  [body(): lax.all_to_all(spectra, ('input', 'freq'), split_axis=0, concat_axis=2, t...]
    all_gather x1 -> x0, waiting for transfers between devices: 60 us -> none  [body(): full = lax.all_gather(local, 'tm', axis=2, tiled=True)]
    all_to_all x0 -> x4, starting transfers between devices: none -> 52.3 us  [body(): lax.all_to_all(block, ('input', 'freq'), split_axis=0, concat_axis=0, til...]
    all_to_all x0 -> x4, waiting for transfers between devices: none -> 31.6 us  [body(): lax.all_to_all(block, ('input', 'freq'), split_axis=0, concat_axis=0, til...]
    ppermute x0 -> x4, waiting for transfers between devices: none -> 31.2 us  [swapped(): return lax.ppermute(block, axis, [(i, size - 1 - i) for i in range(size)])]
    pallas_call x0 -> x11, Pallas kernels: none -> 26.4 us  [the longest x4 12.8 us: correlate(): pl.pallas_call(functools.partial(correlate_kernel, width, scale, result i...]
    dot_general x3 -> x0, matrix products: 24.1 us -> none  [the longest x1 16.4 us: body(): jnp.einsum('rcs,its->cirt', table, filtered, preferred_element_type=jnp.f...]
    another operation x2, other arithmetic: 22.5 us -> 1.79 us
  transfers between devices with their start and end apart: 2 -> 9, of which waited for: 1 -> 6; matrix products, arithmetic and copies ran while one was open for 8% -> 3% of each run, Pallas kernels for 0% -> 9%
where the time goes in v1:
time: 166 us; the launch traced here: 163 us
  waiting for transfers between devices  63.6 us (38%)
  starting transfers between devices  59.2 us (36%)
  Pallas kernels  26.4 us (16%)
  local copies, waits for them, and re-layouts  8.76 us (5%)
  other arithmetic  5 us (3%)
    all_to_all x4, starting transfers between devices, body(): lax.all_to_all(block, ('input', 'freq'), split_axis=0, concat_axis=0, til...  52.3 us
    all_to_all x4, waiting for transfers between devices, body(): lax.all_to_all(block, ('input', 'freq'), split_axis=0, concat_axis=0, til...  31.6 us
    ppermute x4, waiting for transfers between devices, swapped(): return lax.ppermute(block, axis, [(i, size - 1 - i) for i in range(size)])  31.2 us
    pallas_call x4, Pallas kernels, correlate(): pl.pallas_call(functools.partial(correlate_kernel, width, scale, result i...  12.8 us
    unnamed x20, local copies, waits for them, and re-layouts  7.37 us
    pallas_call x1, Pallas kernels, filter_bank(): pl.pallas_call(filter_kernel, grid=(width,), in_specs=[pl.BlockSpec((1, c...  7.3 us
    pallas_call x4, Pallas kernels, spectra(): pl.pallas_call(functools.partial(spectra_kernel, width), out_shape=jax.Sh...  6.26 us
    ppermute x1, starting transfers between devices, passed_along(): return lax.ppermute(block, axis, route)  3.49 us
  transfers between devices with their start and end apart: 9, of which 6 were waited for; matrix products, arithmetic and copies ran while one was open for 3% of the time, Pallas kernels for 9%

profile of v1, /device:TPU:38, one launch (start us, length us, event | category | flops | bytes accessed | tf_op | source)
XLA Modules:
  0.0 163.1 jit_solution(14257797370656500164)
XLA Ops:
  0.0 1.0 slice.3
  1.0 3.5 %collective-permute-start = (bf16[8,4,2048]{2,1,0:T(4,128)(2,1)S(1)}, bf16[8,4,2048]{2,1,0:T(4,128)(2,1)S(1)}, u32[]{:S(2)}, u32[]{:S(2)}) collective-permute-start(bf16[8,4,2048]{2,1,0:T(4,128)(2,1)S(1)} %slice.3), channel_id=1, source_target_pairs={{0,1},{2,3},{4,5},{6,7},{8,9},{10,11},{12,13},{14,15},{16,17},{18,... | collective-permute-start | bytes 393224 | tf_op jit(solution)/shard_map/ppermute | solution.py:19
  4.6 1.1 fusion.6
  6.5 0.8 collective-permute-done.hist_ref
  8.0 7.3 %filter_bank.1 = (bf16[1024,512]{1,0:T(8,128)(2,1)S(1)}, bf16[1024,512]{1,0:T(8,128)(2,1)S(1)}, bf16[1024,1024]{1,0:T(8,128)(2,1)S(1)}) custom-call(bf16[8,128,2048]{2,1,0:T(8,128)(2,1)} %volt_ref.1, bf16[8,4,2048]{2,1,0:T(4,128)(2,1)S(1)} %collective-permute-done.hist_ref, f32[4,2048]{1,0:T(4,128)S(1)} %copy-done.8), custom_call_target="tpu_custom_call" | custom-call | flops 41943040 | bytes 8388608 | tf_op jit(solution)/shard_map/filter_bank/pallas_call | solution.py:84
  15.3 1.0 copy-done.6
  16.3 1.9 %spectra.7 = bf16[128,16,128]{2,1,0:T(8,128)(2,1)} custom-call(bf16[256,512]{1,0:T(8,128)(2,1)S(1)} %pad_maximum_fusion.3.table_ref, bf16[1024,512]{1,0:T(8,128)(2,1)S(1)} %get-tuple-element.14.filt_ref), custom_call_target="tpu_custom_call" | custom-call | flops 268435456 | bytes 1048576 | tf_op jit(solution)/shard_map/spectra/pallas_call | solution.py:122
  18.2 14.8 %all-to-all-start.2 = ((bf16[128,16,128]{2,1,0:T(8,128)(2,1)}), bf16[128,16,128]{2,1,0:T(8,128)(2,1)S(1)}, u32[]{:S(2)}, u32[]{:S(2)}) async-start(bf16[128,16,128]{2,1,0:T(8,128)(2,1)} %spectra.7), calls=%async_computation.2 | async-start | bytes 1048576 | tf_op jit(solution)/shard_map/all_to_all | solution.py:224
  33.7 1.0 subtract_convert_fusion
  34.8 2.0 %spectra.5 = bf16[128,16,128]{2,1,0:T(8,128)(2,1)} custom-call(bf16[256,1024]{1,0:T(8,128)(2,1)S(1)} %pad_maximum_fusion.1.table_ref, bf16[1024,1024]{1,0:T(8,128)(2,1)S(1)} %get-tuple-element.12.filt_ref), custom_call_target="tpu_custom_call" | custom-call | flops 536870912 | bytes 2097152 | tf_op jit(solution)/shard_map/spectra/pallas_call | solution.py:122
  36.8 14.2 %all-to-all-done.2.refs_1_ = bf16[128,16,128]{2,1,0:T(8,128)(2,1)S(1)} async-done(((bf16[128,16,128]{2,1,0:T(8,128)(2,1)}), bf16[128,16,128]{2,1,0:T(8,128)(2,1)S(1)}, u32[]{:S(2)}, u32[]{:S(2)}) %all-to-all-start.2) | async-done | bytes 524320 | tf_op jit(solution)/shard_map/all_to_all | solution.py:224
  51.1 9.2 %all-to-all-start = ((bf16[128,16,128]{2,1,0:T(8,128)(2,1)}), bf16[128,16,128]{2,1,0:T(8,128)(2,1)}, u32[]{:S(2)}, u32[]{:S(2)}) async-start(bf16[128,16,128]{2,1,0:T(8,128)(2,1)} %spectra.5), calls=%async_computation | async-start | bytes 1048576 | tf_op jit(solution)/shard_map/all_to_all | solution.py:224
  60.3 2.0 %collective-permute-start.3 = (bf16[128,16,128]{2,1,0:T(8,128)(2,1)S(1)}, bf16[128,16,128]{2,1,0:T(8,128)(2,1)S(1)}, u32[]{:S(2)}, u32[]{:S(2)}) collective-permute-start(bf16[128,16,128]{2,1,0:T(8,128)(2,1)S(1)} %all-to-all-done.2.refs_1_), channel_id=1, source_target_pairs={{0,1},{1,0},{2,3},{3,2},{4,5},{5,4},{6,7},{7,6},{8,9},{9,8},{10,11... | collective-permute-start | bytes 1572872 | tf_op jit(solution)/shard_map/ppermute | solution.py:24
  62.3 0.9 pad_maximum_fusion.2.table_ref
  63.2 1.2 copy-done.7
  64.4 1.1 spectra.6.refs_0_
  65.5 0.8 copy-done
  66.3 13.3 %collective-permute-done.3.refs_1_.refs_2_ = bf16[128,16,128]{2,1,0:T(8,128)(2,1)S(1)} collective-permute-done((bf16[128,16,128]{2,1,0:T(8,128)(2,1)S(1)}, bf16[128,16,128]{2,1,0:T(8,128)(2,1)S(1)}, u32[]{:S(2)}, u32[]{:S(2)}) %collective-permute-start.3) | collective-permute-done | bytes 524320 | tf_op jit(solution)/shard_map/ppermute | solution.py:24
  79.7 0.8 copy-done.2
  80.5 14.6 %all-to-all-start.3 = ((bf16[128,16,128]{2,1,0:T(8,128)(2,1)}), bf16[128,16,128]{2,1,0:T(8,128)(2,1)}, u32[]{:S(2)}, u32[]{:S(2)}) async-start(bf16[128,16,128]{2,1,0:T(8,128)(2,1)} %after.3), calls=%async_computation.3 | async-start | bytes 1048576 | tf_op jit(solution)/shard_map/all_to_all | solution.py:224
  95.2 1.0 pad_maximum_fusion.table_ref
  96.2 1.2 spectra.4.refs_0_
  98.2 15.2 %collective-permute-done.1.refs_1_.refs_2_ = bf16[128,16,128]{2,1,0:T(8,128)(2,1)S(1)} collective-permute-done((bf16[128,16,128]{2,1,0:T(8,128)(2,1)}, bf16[128,16,128]{2,1,0:T(8,128)(2,1)S(1)}, u32[]{:S(2)}, u32[]{:S(2)}) %collective-permute-start.1) | collective-permute-done | bytes 524320 | tf_op jit(solution)/shard_map/ppermute | solution.py:24
  113.4 0.8 copy-done.4
  114.2 13.7 %all-to-all-start.1 = ((bf16[128,16,128]{2,1,0:T(8,128)(2,1)}), bf16[128,16,128]{2,1,0:T(8,128)(2,1)S(1)}, u32[]{:S(2)}, u32[]{:S(2)}) async-start(bf16[128,16,128]{2,1,0:T(8,128)(2,1)} %after.2), calls=%async_computation.1 | async-start | bytes 1048576 | tf_op jit(solution)/shard_map/all_to_all | solution.py:224
  128.6 17.3 %all-to-all-done.1.refs_1_ = bf16[128,16,128]{2,1,0:T(8,128)(2,1)S(1)} async-done(((bf16[128,16,128]{2,1,0:T(8,128)(2,1)}), bf16[128,16,128]{2,1,0:T(8,128)(2,1)S(1)}, u32[]{:S(2)}, u32[]{:S(2)}) %all-to-all-start.1) | async-done | bytes 524320 | tf_op jit(solution)/shard_map/all_to_all | solution.py:224
  146.5 1.0 copy-done.3
  147.6 2.7 %correlate.4.refs_3_ = bf16[2,4,512,1024]{3,2,1,0:T(8,128)(2,1)} custom-call(s32[1]{0:T(128)} %bitcast.refs_0_, bf16[128,16,128]{2,1,0:T(8,128)(2,1)S(1)} %all-to-all-done.2.refs_1_, bf16[128,16,128]{2,1,0:T(8,128)(2,1)S(1)} %copy-done.3), custom_call_target="tpu_custom_call" | custom-call | flops 1073741824 | bytes 2097152 | tf_op jit(solution)/shard_map/correlate/pallas_call | solution.py:177
  150.3 3.7 %correlate.5.refs_3_ = bf16[2,4,512,1024]{3,2,1,0:T(8,128)(2,1)} custom-call(s32[1]{0:T(128)} %bitcast.refs_0_, bf16[128,16,128]{2,1,0:T(8,128)(2,1)} %all-to-all-done.refs_1_, bf16[128,16,128]{2,1,0:T(8,128)(2,1)S(1)} %copy-done.5, bf16[2,4,512,1024]{3,2,1,0:T(8,128)(2,1)} %correlate.4.refs_3_), custom_call_target="tpu_custom_call", output_to_operand_aliasing={{}: (3, {})} | custom-call | flops 1073741824 | bytes 2097152 | tf_op jit(solution)/shard_map/correlate/pallas_call | solution.py:177
  154.0 3.7 %correlate.6.refs_3_ = bf16[2,4,512,1024]{3,2,1,0:T(8,128)(2,1)} custom-call(s32[1]{0:T(128)} %bitcast.refs_0_, bf16[128,16,128]{2,1,0:T(8,128)(2,1)} %all-to-all-done.3.refs_1_, bf16[128,16,128]{2,1,0:T(8,128)(2,1)S(1)} %collective-permute-done.4.refs_2_, bf16[2,4,512,1024]{3,2,1,0:T(8,128)(2,1)} %correlate.5.refs_3_), custom_call_target="tpu_custom_call", output_to_operand_aliasing={{}: (3, {})} | custom-call | flops 1073741824 | bytes 2097152 | tf_op jit(solution)/shard_map/correlate/pallas_call | solution.py:177
  157.7 2.7 %collective-permute-done.2.refs_2_ = bf16[128,16,128]{2,1,0:T(8,128)(2,1)S(1)} collective-permute-done((bf16[128,16,128]{2,1,0:T(8,128)(2,1)S(1)}, bf16[128,16,128]{2,1,0:T(8,128)(2,1)S(1)}, u32[]{:S(2)}, u32[]{:S(2)}) %collective-permute-start.2) | collective-permute-done | bytes 524320 | tf_op jit(solution)/shard_map/ppermute | solution.py:24
  160.4 2.7 %correlate.7 = bf16[2,4,512,1024]{3,2,1,0:T(8,128)(2,1)} custom-call(s32[1]{0:T(128)} %bitcast.refs_0_, bf16[128,16,128]{2,1,0:T(8,128)(2,1)S(1)} %all-to-all-done.1.refs_1_, bf16[128,16,128]{2,1,0:T(8,128)(2,1)S(1)} %collective-permute-done.2.refs_2_, bf16[2,4,512,1024]{3,2,1,0:T(8,128)(2,1)} %correlate.6.refs_3_), custom_call_target="tpu_custom_call", output_to_operand_aliasing={{}: (3, {})} | custom-call | flops 1073741824 | bytes 2097152 | tf_op jit(solution)/shard_map/correlate/pallas_call | solution.py:177
  (31 shorter events, 4.5 us)
Async XLA Ops:
  1.0 6.2 %collective-permute-start = (bf16[8,4,2048]{2,1,0:T(4,128)(2,1)S(1)}, bf16[8,4,2048]{2,1,0:T(4,128)(2,1)S(1)}, u32[]{:S(2)}, u32[]{:S(2)}) collective-permute-start(bf16[8,4,2048]{2,1,0:T(4,128)(2,1)S(1)} %slice.3), channel_id=1, source_target_pairs={{0,1},{2,3},{4,5},{6,7},{8,9},{10,11},{12,13},{14,15},{16,17},{18,... | collective-permute-start | bytes 393224 | tf_op jit(solution)/shard_map/ppermute | solution.py:19
  7.3 0.8 copy-start.8
  15.3 1.0 copy-start.6
  18.2 32.9 %all-to-all-start.2 = ((bf16[128,16,128]{2,1,0:T(8,128)(2,1)}), bf16[128,16,128]{2,1,0:T(8,128)(2,1)S(1)}, u32[]{:S(2)}, u32[]{:S(2)}) async-start(bf16[128,16,128]{2,1,0:T(8,128)(2,1)} %spectra.7), calls=%async_computation.2 | async-start | bytes 1048576 | tf_op jit(solution)/shard_map/all_to_all | solution.py:224
  51.1 29.4 %all-to-all-start = ((bf16[128,16,128]{2,1,0:T(8,128)(2,1)}), bf16[128,16,128]{2,1,0:T(8,128)(2,1)}, u32[]{:S(2)}, u32[]{:S(2)}) async-start(bf16[128,16,128]{2,1,0:T(8,128)(2,1)} %spectra.5), calls=%async_computation | async-start | bytes 1048576 | tf_op jit(solution)/shard_map/all_to_all | solution.py:224
  60.3 19.3 %collective-permute-start.3 = (bf16[128,16,128]{2,1,0:T(8,128)(2,1)S(1)}, bf16[128,16,128]{2,1,0:T(8,128)(2,1)S(1)}, u32[]{:S(2)}, u32[]{:S(2)}) collective-permute-start(bf16[128,16,128]{2,1,0:T(8,128)(2,1)S(1)} %all-to-all-done.2.refs_1_), channel_id=1, source_target_pairs={{0,1},{1,0},{2,3},{3,2},{4,5},{5,4},{6,7},{7,6},{8,9},{9,8},{10,11... | collective-permute-start | bytes 1572872 | tf_op jit(solution)/shard_map/ppermute | solution.py:24
  63.2 1.2 copy-start.7
  65.5 0.8 copy-start
  79.7 0.8 copy-start.2
  80.5 33.7 %all-to-all-start.3 = ((bf16[128,16,128]{2,1,0:T(8,128)(2,1)}), bf16[128,16,128]{2,1,0:T(8,128)(2,1)}, u32[]{:S(2)}, u32[]{:S(2)}) async-start(bf16[128,16,128]{2,1,0:T(8,128)(2,1)} %after.3), calls=%async_computation.3 | async-start | bytes 1048576 | tf_op jit(solution)/shard_map/all_to_all | solution.py:224
  95.1 18.4 %collective-permute-start.1 = (bf16[128,16,128]{2,1,0:T(8,128)(2,1)}, bf16[128,16,128]{2,1,0:T(8,128)(2,1)S(1)}, u32[]{:S(2)}, u32[]{:S(2)}) collective-permute-start(bf16[128,16,128]{2,1,0:T(8,128)(2,1)} %all-to-all-done.refs_1_), channel_id=1, source_target_pairs={{0,1},{1,0},{2,3},{3,2},{4,5},{5,4},{6,7},{7,6},{8,9},{9,8},{10,11... | collective-permute-start | bytes 1572872 | tf_op jit(solution)/shard_map/ppermute | solution.py:24
  97.4 0.8 copy-start.1
  113.4 0.8 copy-start.4
  114.2 36.1 %copy-start.5 = (bf16[128,16,128]{2,1,0:T(8,128)(2,1)S(1)}, bf16[128,16,128]{2,1,0:T(8,128)(2,1)}, u32[]{:S(2)}) copy-start(bf16[128,16,128]{2,1,0:T(8,128)(2,1)} %copy-done.4) | copy-start | bytes 1572868
  114.2 31.7 %all-to-all-start.1 = ((bf16[128,16,128]{2,1,0:T(8,128)(2,1)}), bf16[128,16,128]{2,1,0:T(8,128)(2,1)S(1)}, u32[]{:S(2)}, u32[]{:S(2)}) async-start(bf16[128,16,128]{2,1,0:T(8,128)(2,1)} %after.2), calls=%async_computation.1 | async-start | bytes 1048576 | tf_op jit(solution)/shard_map/all_to_all | solution.py:224
  127.9 26.1 %collective-permute-start.4 = (bf16[128,16,128]{2,1,0:T(8,128)(2,1)}, bf16[128,16,128]{2,1,0:T(8,128)(2,1)S(1)}, u32[]{:S(2)}, u32[]{:S(2)}) collective-permute-start(bf16[128,16,128]{2,1,0:T(8,128)(2,1)} %all-to-all-done.3.refs_1_), channel_id=1, source_target_pairs={{0,1},{1,0},{2,3},{3,2},{4,5},{5,4},{6,7},{7,6},{8,9},{9,8},{10,11... | collective-permute-start | bytes 1572872 | tf_op jit(solution)/shard_map/ppermute | solution.py:24
  145.9 14.5 %collective-permute-start.2 = (bf16[128,16,128]{2,1,0:T(8,128)(2,1)S(1)}, bf16[128,16,128]{2,1,0:T(8,128)(2,1)S(1)}, u32[]{:S(2)}, u32[]{:S(2)}) collective-permute-start(bf16[128,16,128]{2,1,0:T(8,128)(2,1)S(1)} %all-to-all-done.1.refs_1_), channel_id=1, source_target_pairs={{0,1},{1,0},{2,3},{3,2},{4,5},{5,4},{6,7},{7,6},{8,9},{9,8},{10,11... | collective-permute-start | bytes 1572872 | tf_op jit(solution)/shard_map/ppermute | solution.py:24
  146.5 1.0 copy-start.3

commit v2 on v1

v2 whole, which is shorter than its diff:
```python
import functools
import math

import jax
import jax.numpy as jnp
from jax import lax
from jax.experimental import pallas as pl
from jax.experimental.pallas import tpu as pltpu
from jax.sharding import PartitionSpec as P

CH = 512
LANES = 128
ROWS = 32
MIB = 1024 * 1024


def passed_along(block, axis, distance):
    devices = range(lax.axis_size(axis))
    route = [(i - distance, i) for i in devices if i - distance in devices]
    return lax.ppermute(block, axis, route)


def swapped(block, axis):
    size = lax.axis_size(axis)
    return lax.ppermute(block, axis, [(i, size - 1 - i) for i in range(size)])


def tables(npoints, order, stride, per_group):
    half, quarter = npoints // 2, npoints // 4
    unit = 2.0 * math.pi / npoints
    sample = lax.broadcasted_iota(jnp.int32, (order.shape[0], quarter), 1)
    angle = ((stride * order[:, None] * sample) % npoints).astype(jnp.float32) * unit
    cos_base, sin_base = jnp.cos(angle), jnp.sin(angle)
    cos_base, sin_base = lax.optimization_barrier((cos_base, sin_base))
    out = [jnp.concatenate([cos_base, -sin_base]).astype(jnp.bfloat16)]
    for j in range(1, per_group):
        depth = quarter if j % 2 == 0 else half
        turn = ((j * jnp.arange(depth, dtype=jnp.int32)) % npoints).astype(jnp.float32) * unit
        cos_turn, sin_turn = jnp.cos(turn), jnp.sin(turn)
        cos_wide = jnp.tile(cos_base, (1, depth // quarter))
        sin_wide = jnp.tile(sin_base, (1, depth // quarter))
        real = cos_wide * cos_turn - sin_wide * sin_turn
        imag = -(sin_wide * cos_turn + cos_wide * sin_turn)
        out.append(jnp.concatenate([real, imag]).astype(jnp.bfloat16))
    return out


def filter_kernel(volt_ref, hist_ref, taps_ref, sum_ref, alt_ref, diff_ref, wide_ref):
    ntaps = taps_ref.shape[0]
    width, count, _ = volt_ref.shape
    quarter = sum_ref.shape[1]
    nhist = hist_ref.shape[1]
    pad = 8
    rows = min(ROWS, count)

    @pl.loop(0, width)
    def _(i):
        for start in range(0, quarter, LANES):
            places = [slice(start + slot * quarter, start + slot * quarter + LANES) for slot in range(4)]
            for slot, lanes in enumerate(places):
                wide_ref[slot, pad - nhist : pad] = hist_ref[i, :, lanes].astype(jnp.float32)
                wide_ref[slot, pad:] = volt_ref[i, :, lanes].astype(jnp.float32)
            for top in range(0, count, rows):
                here = pl.ds(pl.multiple_of(i * count + top, rows), rows)

                def filtered(slot):
                    total = taps_ref[0, places[slot]] * wide_ref[slot, pad + top : pad + top + rows]
                    for lag in range(1, ntaps):
                        first = pad + top - lag
                        total = total + taps_ref[lag, places[slot]] * wide_ref[slot, first : first + rows]
                    return total

                first, third = filtered(0), filtered(2)
                diff_ref[here, places[0]] = (first - third).astype(jnp.bfloat16)
                even = first + third
                second, fourth = filtered(1), filtered(3)
                diff_ref[here, places[1]] = (second - fourth).astype(jnp.bfloat16)
                odd = second + fourth
                sum_ref[here, places[0]] = (even + odd).astype(jnp.bfloat16)
                alt_ref[here, places[0]] = (even - odd).astype(jnp.bfloat16)


def filter_bank(voltages, history, taps):
    width, count, npoints = voltages.shape
    half, quarter = npoints // 2, npoints // 4
    rows = width * count
    depths = (quarter, quarter, half)
    return pl.pallas_call(
        filter_kernel,
        in_specs=[pl.BlockSpec(memory_space=pltpu.VMEM)] * 3,
        out_specs=[pl.BlockSpec(memory_space=pltpu.VMEM)] * 3,
        out_shape=[jax.ShapeDtypeStruct((rows, d), jnp.bfloat16) for d in depths],
        scratch_shapes=[pltpu.VMEM((4, 8 + count, LANES), jnp.float32)],
        compiler_params=pltpu.CompilerParams(vmem_limit_bytes=24 * MIB),
        cost_estimate=pl.CostEstimate(flops=20 * rows * npoints, bytes_accessed=4 * rows * npoints, transcendentals=0),
        name="filter_bank",
    )(voltages, history, taps)


def spectra_kernel(width, table_ref, filt_ref, keep_ref, send_ref, wide_ref):
    rows = filt_ref.shape[0]
    count = rows // width
    groups = keep_ref.shape[0]
    pair = 2 * count
    for step in range(rows // pair):
        product = lax.dot_general(
            table_ref[...], filt_ref[step * pair : (step + 1) * pair, :],
            (((1,), (1,)), ((), ())), preferred_element_type=jnp.float32,
        )
        wide_ref[2 * step] = product[:, :count]
        wide_ref[2 * step + 1] = product[:, count:]

    for at, ref in enumerate((keep_ref, send_ref)):
        for g in range(groups):
            real = wide_ref[:, at * groups + g, :]
            imag = wide_ref[:, (2 + at) * groups + g, :]
            ref[g] = jnp.concatenate([real, imag], axis=0).astype(jnp.bfloat16)


def spectra(table, filt, width, groups):
    rows, depth = filt.shape
    count = rows // width
    return pl.pallas_call(
        functools.partial(spectra_kernel, width),
        out_shape=[jax.ShapeDtypeStruct((groups, 2 * width, count), jnp.bfloat16)] * 2,
        in_specs=[pl.BlockSpec(memory_space=pltpu.VMEM)] * 2,
        out_specs=[pl.BlockSpec(memory_space=pltpu.VMEM)] * 2,
        scratch_shapes=[pltpu.VMEM((width, 4 * groups, count), jnp.float32)],
        compiler_params=pltpu.CompilerParams(vmem_limit_bytes=24 * MIB),
        cost_estimate=pl.CostEstimate(
            flops=8 * groups * rows * depth, bytes_accessed=2 * rows * depth, transcendentals=0
        ),
        name="spectra",
    )(table, filt)


def merge_kernel(units, place_ref, *refs):
    arrays = 2 * len({at for at, _ in units})
    outs = refs[arrays:]
    groups, _, rows, count = outs[0].shape
    width = rows // 2
    low = place_ref[2] == 0
    for side, out_ref in enumerate(outs):
        first_group = 0 if len(outs) == 1 else jnp.bitwise_xor(place_ref[1], side) * groups
        for to, (at, part) in enumerate(units):
            these = (pl.ds(first_group, groups), slice(part * width, (part + 1) * width))
            own = refs[at][these].astype(jnp.float32)
            other = refs[arrays // 2 + at][these].astype(jnp.float32)
            first, second = jnp.where(low, own, other), jnp.where(low, other, own)
            out_ref[:, to] = jnp.concatenate([first, second], axis=1).astype(jnp.bfloat16)


def merge(place, units, own, other, sides):
    channels = sorted({j for j, _ in units})
    places = tuple((channels.index(j), part) for j, part in units)
    arrays = [own[j] for j in channels] + [other[j] for j in channels]
    groups, rows, count = arrays[0].shape
    return pl.pallas_call(
        functools.partial(merge_kernel, places),
        out_shape=[jax.ShapeDtypeStruct((groups // sides, len(units), rows, count), jnp.bfloat16)] * sides,
        in_specs=[pl.BlockSpec(memory_space=pltpu.SMEM)] + [pl.BlockSpec(memory_space=pltpu.VMEM)] * len(arrays),
        out_specs=[pl.BlockSpec(memory_space=pltpu.VMEM)] * sides,
        compiler_params=pltpu.CompilerParams(vmem_limit_bytes=24 * MIB),
        cost_estimate=pl.CostEstimate(
            flops=0, bytes_accessed=4 * len(units) * groups * rows * count, transcendentals=0
        ),
        name="merge",
    )(place, *arrays)


def correlate_kernel(scale, place_ref, *refs):
    out_ref, all_ref, turned_ref = refs[-3:]
    count = refs[0].shape[-1]
    inputs = all_ref.shape[0]
    step = out_ref.shape[2]
    rows = turned_ref.shape[0]
    start = pl.multiple_of(place_ref[0] * rows, rows)

    @pl.when(pl.program_id(0) == 0)
    def _():
        for at in range(4):
            ref = refs[at]
            sides = 1 if len(ref.shape) == 4 else ref.shape[1]
            extent = inputs // sides
            for side in range(sides):
                slot = at ^ side
                lanes = slice(slot * count, (slot + 1) * count)
                if sides == 1:
                    all_ref[:, lanes] = ref[:, 0].reshape(extent, count)
                else:
                    first = jnp.bitwise_xor(place_ref[1], side) * extent
                    here = pl.ds(pl.multiple_of(first, extent), extent)
                    all_ref[here, lanes] = ref[:, side, 0].reshape(extent, count)
        half = 2 * count
        turned_ref[:, :half] = all_ref[pl.ds(start, rows), half:]
        turned_ref[:, half:] = -all_ref[pl.ds(start, rows), :half]

    here = pl.multiple_of(pl.program_id(0) * step, step)
    dot = functools.partial(
        lax.dot_general, dimension_numbers=(((1,), (1,)), ((), ())), preferred_element_type=jnp.float32
    )
    left = all_ref[pl.ds(start + here, step), :]
    out_ref[0, 0] = (dot(left, all_ref[...]) * scale).astype(jnp.bfloat16)
    left = turned_ref[pl.ds(here, step), :]
    out_ref[1, 0] = (dot(left, all_ref[...]) * scale).astype(jnp.bfloat16)


def correlate(place, pieces, result, channel, channels, inputs, parts):
    count = pieces[0][0].shape[-1]
    rows = inputs // parts
    step = min(256, rows)
    scale = 1.0 / (parts * count)
    args = [place]
    in_specs = [pl.BlockSpec(memory_space=pltpu.SMEM)]
    for array, unit in pieces:
        args.append(array)
        lead = array.shape[:-3]
        index = (0,) * len(lead) + (unit, 0, 0)
        in_specs.append(pl.BlockSpec(lead + (1,) + array.shape[-2:], lambda i, index=index: index))
    aliases = {}
    if result is not None:
        aliases = {len(args): 0}
        args.append(result)
        in_specs.append(pl.BlockSpec(memory_space=pl.ANY))
    return pl.pallas_call(
        functools.partial(correlate_kernel, scale),
        grid=(rows // step,),
        in_specs=in_specs,
        out_specs=pl.BlockSpec((2, 1, step, inputs), lambda i: (0, channel, i, 0)),
        out_shape=jax.ShapeDtypeStruct((2, channels, rows, inputs), jnp.bfloat16),
        scratch_shapes=[
            pltpu.VMEM((inputs, 2 * parts * count), jnp.bfloat16),
            pltpu.VMEM((rows, 2 * parts * count), jnp.bfloat16),
        ],
        input_output_aliases=aliases,
        compiler_params=pltpu.CompilerParams(vmem_limit_bytes=24 * MIB),
        cost_estimate=pl.CostEstimate(
            flops=8 * rows * inputs * parts * count, bytes_accessed=4 * rows * inputs, transcendentals=0
        ),
        name="correlate",
    )(*args)


CHUNKS = (((0, 0), (0, 1), (2, 0), (2, 1), (1, 0)), ((1, 1), (3, 0), (3, 1)))
SPLIT = 1


def body(voltages, taps):
    width, count, npoints = voltages.shape
    parts = lax.axis_size("tm")
    groups = lax.axis_size("yh") * lax.axis_size("x") * lax.axis_size("chip")
    cores = lax.axis_size("core")
    per_group = CH // (groups * cores)
    history = passed_along(voltages[:, count - 4 :, :], "tm", 1)
    core = lax.axis_index("core").astype(jnp.int32)
    place = jnp.stack([lax.axis_index("tm").astype(jnp.int32), lax.axis_index("yh").astype(jnp.int32), core])
    half = cores * jnp.arange(groups, dtype=jnp.int32)
    table = tables(npoints, jnp.concatenate([half + core, half + (1 - core)]), per_group, per_group)
    sums, alts, diffs = filter_bank(voltages, history, taps)
    sources = [sums, diffs, alts, diffs]
    own, other, arrived = {}, {}, {}
    for n, units in enumerate(CHUNKS):
        for j in sorted({j for j, _ in units} - set(own)):
            own[j], send = spectra(table[j], sources[j], width, groups)
            other[j] = swapped(send, "core")
        if n == 0:
            (block,) = merge(place, units, own, other, 1)
            axes = ("yh", "x", "chip")
        else:
            here, across = merge(place, units, own, other, 2)
            across = swapped(across, ("yh", "tm"))
            block = jnp.stack([here, across], axis=1)
            axes = ("x", "chip")
        block = lax.all_to_all(block, axes, split_axis=0, concat_axis=0, tiled=True)
        split = SPLIT if n else len(units)
        for first, last in ((0, split), (split, len(units))):
            if first == last:
                continue
            far = block if n == 0 else block[:, :, first:last]
            far = swapped(far, "tm")
            for at in range(first, last):
                arrived[units[at]] = [(block, at), (far, at - first)]
    result = None
    inputs = groups * cores * width
    for j in (0, 2, 1, 3):
        result = correlate(place, arrived[j, 0] + arrived[j, 1], result, j, per_group, inputs, parts)
    return result


def solution(mesh):
    sizes = dict(mesh.shape)
    shape = (2, sizes["input"] // 2, sizes["freq"] // 2, 2, sizes["tm"])
    fine = jax.sharding.Mesh(mesh.devices.reshape(shape), ("yh", "x", "chip", "core", "tm"))
    in_specs = (P(("yh", "x", "chip", "core"), "tm", None), P())
    out_specs = P(None, ("yh", "x", "chip", "core"), "tm", None)
    return jax.shard_map(body, mesh=fine, in_specs=in_specs, out_specs=out_specs, check_vma=False)
```

time: 166 us -> 131 us (0.79); the launches traced: 163 us -> 130 us
  starting transfers between devices: 59.2 us -> 29.7 us
  local copies, waits for them, and re-layouts: 8.76 us -> 5.27 us
  waiting for transfers between devices: 63.6 us -> 65.5 us
    all_to_all x4 -> x2, starting transfers between devices: 52.3 us -> 19.5 us  [body(): block = lax.all_to_all(block, axes, split_axis=0, concat_axis=0, tiled=True)]
    ppermute x4 -> x8, waiting for transfers between devices: 31.2 us -> 36.2 us  [swapped(): return lax.ppermute(block, axis, [(i, size - 1 - i) for i in range(size)])]
    unnamed x20 -> x16, local copies, waits for them, and re-layouts: 7.37 us -> 3.81 us
    ppermute x4 -> x8, starting transfers between devices: 3.35 us -> 6.67 us  [swapped(): return lax.ppermute(block, axis, [(i, size - 1 - i) for i in range(size)])]
    all_to_all x4 -> x2, waiting for transfers between devices: 31.6 us -> 29.3 us  [body(): block = lax.all_to_all(block, axes, split_axis=0, concat_axis=0, tiled=True)]
  transfers between devices with their start and end apart: 9 -> 11, of which waited for: 6 -> 7; matrix products, arithmetic and copies ran while one was open for 3% -> 4% of each run, Pallas kernels for 9% -> 12%
where the time goes in v2:
time: 131 us; the launch traced here: 130 us
  waiting for transfers between devices  65.5 us (50%)
  starting transfers between devices  29.7 us (23%)
  Pallas kernels  25 us (19%)
  local copies, waits for them, and re-layouts  5.27 us (4%)
  other arithmetic  4.7 us (4%)
    ppermute x8, waiting for transfers between devices, swapped(): return lax.ppermute(block, axis, [(i, size - 1 - i) for i in range(size)])  36.2 us
    all_to_all x2, waiting for transfers between devices, body(): block = lax.all_to_all(block, axes, split_axis=0, concat_axis=0, tiled=True)  29.3 us
    all_to_all x2, starting transfers between devices, body(): block = lax.all_to_all(block, axes, split_axis=0, concat_axis=0, tiled=True)  19.5 us
    pallas_call x4, Pallas kernels, correlate(): pl.pallas_call(functools.partial(correlate_kernel, scale), grid=(rows //...  13 us
    pallas_call x4, Pallas kernels, spectra(): pl.pallas_call(functools.partial(spectra_kernel, width), out_shape=[jax.S...  6.81 us
    ppermute x8, starting transfers between devices, swapped(): return lax.ppermute(block, axis, [(i, size - 1 - i) for i in range(size)])  6.67 us
    unnamed x16, local copies, waits for them, and re-layouts  3.81 us
    ppermute x1, starting transfers between devices, passed_along(): return lax.ppermute(block, axis, route)  3.49 us
  transfers between devices with their start and end apart: 11, of which 7 were waited for; matrix products, arithmetic and copies ran while one was open for 4% of the time, Pallas kernels for 12%

profile of v2, /device:TPU:38, one launch (start us, length us, event | category | flops | bytes accessed | tf_op | source)
XLA Modules:
  0.0 130.4 jit_solution(17395770725360391413)
XLA Ops:
  0.0 1.0 slice.9
  1.0 3.5 %collective-permute-start = (bf16[8,4,2048]{2,1,0:T(4,128)(2,1)S(1)}, bf16[8,4,2048]{2,1,0:T(4,128)(2,1)S(1)}, u32[]{:S(2)}, u32[]{:S(2)}) collective-permute-start(bf16[8,4,2048]{2,1,0:T(4,128)(2,1)S(1)} %slice.9), channel_id=1, source_target_pairs={{0,1},{2,3},{4,5},{6,7},{8,9},{10,11},{12,13},{14,15},{16,17},{18,... | collective-permute-start | bytes 393224 | tf_op jit(solution)/shard_map/ppermute | solution.py:20
  4.8 1.1 fusion.6
  6.6 1.1 subtract_convert_fusion
  8.4 3.3 %filter_bank.1 = (bf16[1024,512]{1,0:T(8,128)(2,1)S(1)}, bf16[1024,512]{1,0:T(8,128)(2,1)S(1)}, bf16[1024,1024]{1,0:T(8,128)(2,1)S(1)}) custom-call(bf16[8,128,2048]{2,1,0:T(8,128)(2,1)S(1)} %copy-done.1, bf16[8,4,2048]{2,1,0:T(4,128)(2,1)S(1)} %collective-permute-done.hist_ref, f32[4,2048]{1,0:T(4,128)S(1)} %copy-done.6), custom_call_target="tpu_custom_call" | custom-call | flops 41943040 | bytes 8388608 | tf_op jit(solution)/shard_map/filter_bank/pallas_call | solution.py:88
  11.8 1.8 %spectra.7 = (bf16[64,16,128]{2,1,0:T(8,128)(2,1)S(1)}, bf16[64,16,128]{2,1,0:T(8,128)(2,1)}) custom-call(bf16[256,512]{1,0:T(8,128)(2,1)S(1)} %pad_maximum_fusion.4.table_ref, bf16[1024,512]{1,0:T(8,128)(2,1)S(1)} %get-tuple-element.31.filt_ref), custom_call_target="tpu_custom_call" | custom-call | flops 268435456 | bytes 1048576 | tf_op jit(solution)/shard_map/spectra/pallas_call | solution.py:123
  13.6 1.9 %spectra.4 = (bf16[64,16,128]{2,1,0:T(8,128)(2,1)S(1)}, bf16[64,16,128]{2,1,0:T(8,128)(2,1)}) custom-call(bf16[256,1024]{1,0:T(8,128)(2,1)S(1)} %pad_maximum_fusion.1.table_ref, bf16[1024,1024]{1,0:T(8,128)(2,1)S(1)} %get-tuple-element.22.filt_ref), custom_call_target="tpu_custom_call" | custom-call | flops 536870912 | bytes 2097152 | tf_op jit(solution)/shard_map/spectra/pallas_call | solution.py:123
  16.1 1.8 %spectra.6 = (bf16[64,16,128]{2,1,0:T(8,128)(2,1)S(1)}, bf16[64,16,128]{2,1,0:T(8,128)(2,1)}) custom-call(bf16[256,512]{1,0:T(8,128)(2,1)S(1)} %pad_maximum_fusion.3.table_ref, bf16[1024,512]{1,0:T(8,128)(2,1)S(1)} %get-tuple-element.29.filt_ref), custom_call_target="tpu_custom_call" | custom-call | flops 268435456 | bytes 1048576 | tf_op jit(solution)/shard_map/spectra/pallas_call | solution.py:123
  18.0 1.8 %collective-permute-done.5.refs_3_ = bf16[64,16,128]{2,1,0:T(8,128)(2,1)} collective-permute-done((bf16[64,16,128]{2,1,0:T(8,128)(2,1)}, bf16[64,16,128]{2,1,0:T(8,128)(2,1)}, u32[]{:S(2)}, u32[]{:S(2)}) %collective-permute-start.5) | collective-permute-done | bytes 262176 | tf_op jit(solution)/shard_map/ppermute | solution.py:25
  19.8 1.2 merge.3
  20.9 1.0 copy-done
  22.0 13.9 %all-to-all-start.1 = ((bf16[64,5,16,128]{3,2,1,0:T(8,128)(2,1)}), bf16[64,5,16,128]{3,2,1,0:T(8,128)(2,1)S(1)}, u32[]{:S(2)}, u32[]{:S(2)}) async-start(bf16[64,5,16,128]{3,2,1,0:T(8,128)(2,1)} %copy-done), calls=%async_computation.1 | async-start | bytes 2621440 | tf_op jit(solution)/shard_map/all_to_all | solution.py:274
  35.9 1.1 pad_maximum_fusion.2.table_ref
  37.0 1.2 spectra.5
  38.3 1.5 %collective-permute-done.2.refs_3_ = bf16[64,16,128]{2,1,0:T(8,128)(2,1)S(1)} collective-permute-done((bf16[64,16,128]{2,1,0:T(8,128)(2,1)S(1)}, bf16[64,16,128]{2,1,0:T(8,128)(2,1)S(1)}, u32[]{:S(2)}, u32[]{:S(2)}) %collective-permute-start.2) | collective-permute-done | bytes 262176 | tf_op jit(solution)/shard_map/ppermute | solution.py:25
  39.8 0.9 copy-done.3
  40.8 0.9 copy-done.5
  42.4 3.1 %collective-permute-start.3 = (bf16[32,3,16,128]{3,2,1,0:T(8,128)(2,1)S(1)}, bf16[32,3,16,128]{3,2,1,0:T(8,128)(2,1)S(1)}, u32[]{:S(2)}, u32[]{:S(2)}) collective-permute-start(bf16[32,3,16,128]{3,2,1,0:T(8,128)(2,1)S(1)} %get-tuple-element.28), channel_id=1, source_target_pairs={{0,129},{1,128},{128,1},{129,0},{2,131},{3,130},{130,3},{131,2},{4... | collective-permute-start | bytes 1179656 | tf_op jit(solution)/shard_map/ppermute | solution.py:25
  45.5 16.4 %collective-permute-done.3 = bf16[32,3,16,128]{3,2,1,0:T(8,128)(2,1)S(1)} collective-permute-done((bf16[32,3,16,128]{3,2,1,0:T(8,128)(2,1)S(1)}, bf16[32,3,16,128]{3,2,1,0:T(8,128)(2,1)S(1)}, u32[]{:S(2)}, u32[]{:S(2)}) %collective-permute-start.3) | collective-permute-done | bytes 393248 | tf_op jit(solution)/shard_map/ppermute | solution.py:25
  61.9 1.0 pad_maximum_fusion
  62.9 9.3 %all-to-all-done.1.refs_0_.refs_2_ = bf16[64,5,16,128]{3,2,1,0:T(8,128)(2,1)S(1)} async-done(((bf16[64,5,16,128]{3,2,1,0:T(8,128)(2,1)}), bf16[64,5,16,128]{3,2,1,0:T(8,128)(2,1)S(1)}, u32[]{:S(2)}, u32[]{:S(2)}) %all-to-all-start.1) | async-done | bytes 1310752 | tf_op jit(solution)/shard_map/all_to_all | solution.py:274
  72.2 5.6 %all-to-all-start = ((bf16[32,2,3,16,128]{4,3,2,1,0:T(8,128)(2,1)}), bf16[32,2,3,16,128]{4,3,2,1,0:T(8,128)(2,1)S(1)}, u32[]{:S(2)}, u32[]{:S(2)}) async-start(bf16[32,2,3,16,128]{4,3,2,1,0:T(8,128)(2,1)} %pad_maximum_fusion), calls=%async_computation | async-start | bytes 1572864 | tf_op jit(solution)/shard_map/all_to_all | solution.py:274
  77.8 0.8 collective-permute-start.7
  78.6 20.1 %all-to-all-done.refs_2_.refs_0_ = bf16[32,2,3,16,128]{4,3,2,1,0:T(8,128)(2,1)S(1)} async-done(((bf16[32,2,3,16,128]{4,3,2,1,0:T(8,128)(2,1)}), bf16[32,2,3,16,128]{4,3,2,1,0:T(8,128)(2,1)S(1)}, u32[]{:S(2)}, u32[]{:S(2)}) %all-to-all-start) | async-done | bytes 786464 | tf_op jit(solution)/shard_map/all_to_all | solution.py:274
  98.7 0.8 collective-permute-start.4
  99.5 1.4 %collective-permute-start.8 = (bf16[32,2,1,16,128]{4,3,2,1,0:T(8,128)(2,1)S(1)}, bf16[32,2,1,16,128]{4,3,2,1,0:T(8,128)(2,1)S(1)}, u32[]{:S(2)}, u32[]{:S(2)}) collective-permute-start(bf16[32,2,1,16,128]{4,3,2,1,0:T(8,128)(2,1)S(1)} %slice.13), channel_id=1, source_target_pairs={{0,1},{1,0},{2,3},{3,2},{4,5},{5,4},{6,7},{7,6},{8,9},{9,8},{10,11... | collective-permute-start | bytes 786440 | tf_op jit(solution)/shard_map/ppermute | solution.py:25
  100.9 8.7 %collective-permute-done.7.refs_1_.refs_3_ = bf16[64,5,16,128]{3,2,1,0:T(8,128)(2,1)S(1)} collective-permute-done((bf16[64,5,16,128]{3,2,1,0:T(8,128)(2,1)S(1)}, bf16[64,5,16,128]{3,2,1,0:T(8,128)(2,1)S(1)}, u32[]{:S(2)}, u32[]{:S(2)}) %collective-permute-start.7) | collective-permute-done | bytes 1310752 | tf_op jit(solution)/shard_map/ppermute | solution.py:25
  109.6 3.3 %correlate.4.refs_4_ = bf16[2,4,512,1024]{3,2,1,0:T(8,128)(2,1)} custom-call(s32[3]{0:T(128)S(1)} %pad_add_fusion.place_ref, bf16[64,5,16,128]{3,2,1,0:T(8,128)(2,1)S(1)} %all-to-all-done.1.refs_0_.refs_2_, bf16[64,5,16,128]{3,2,1,0:T(8,128)(2,1)S(1)} %collective-permute-done.7.refs_1_.refs_3_, bf16[64,5,16,128]{3,2,1,0:T(8,128)(2,1)S(1)} %all-to-all-done.1.refs_0_.refs_2_, ...), custom_call_target="tpu_custom_call" | custom-call | flops 1073741824 | bytes 2097152 | tf_op jit(solution)/shard_map/correlate/pallas_call | solution.py:225
  112.8 3.3 %correlate.5.refs_4_ = bf16[2,4,512,1024]{3,2,1,0:T(8,128)(2,1)} custom-call(s32[3]{0:T(128)S(1)} %pad_add_fusion.place_ref, bf16[64,5,16,128]{3,2,1,0:T(8,128)(2,1)S(1)} %all-to-all-done.1.refs_0_.refs_2_, bf16[64,5,16,128]{3,2,1,0:T(8,128)(2,1)S(1)} %collective-permute-done.7.refs_1_.refs_3_, ...), custom_call_target="tpu_custom_call", output_to_operand_aliasing={{}: (5, {})} | custom-call | flops 1073741824 | bytes 2097152 | tf_op jit(solution)/shard_map/correlate/pallas_call | solution.py:225
  116.1 7.8 %collective-permute-done.8.refs_3_ = bf16[32,2,1,16,128]{4,3,2,1,0:T(8,128)(2,1)S(1)} collective-permute-done((bf16[32,2,1,16,128]{4,3,2,1,0:T(8,128)(2,1)S(1)}, bf16[32,2,1,16,128]{4,3,2,1,0:T(8,128)(2,1)S(1)}, u32[]{:S(2)}, u32[]{:S(2)}) %collective-permute-start.8) | collective-permute-done | bytes 262176 | tf_op jit(solution)/shard_map/ppermute | solution.py:25
  123.9 3.3 %correlate.6.refs_4_ = bf16[2,4,512,1024]{3,2,1,0:T(8,128)(2,1)} custom-call(s32[3]{0:T(128)S(1)} %pad_add_fusion.place_ref, bf16[64,5,16,128]{3,2,1,0:T(8,128)(2,1)S(1)} %all-to-all-done.1.refs_0_.refs_2_, bf16[64,5,16,128]{3,2,1,0:T(8,128)(2,1)S(1)} %collective-permute-done.7.refs_1_.refs_3_, ...), custom_call_target="tpu_custom_call", output_to_operand_aliasing={{}: (5, {})} | custom-call | flops 1073741824 | bytes 2097152 | tf_op jit(solution)/shard_map/correlate/pallas_call | solution.py:225
  127.2 3.3 %correlate.7 = bf16[2,4,512,1024]{3,2,1,0:T(8,128)(2,1)} custom-call(s32[3]{0:T(128)S(1)} %pad_add_fusion.place_ref, bf16[32,2,3,16,128]{4,3,2,1,0:T(8,128)(2,1)S(1)} %all-to-all-done.refs_2_.refs_0_, bf16[32,2,2,16,128]{4,3,2,1,0:T(8,128)(2,1)S(1)} %collective-permute-done.4.refs_1_.refs_3_, ...), custom_call_target="tpu_custom_call", output_to_operand_aliasing={{}: (5, {})} | custom-call | flops 1073741824 | bytes 2097152 | tf_op jit(solution)/shard_map/correlate/pallas_call | solution.py:225
  (36 shorter events, 3.1 us)
Async XLA Ops:
  1.0 6.8 %collective-permute-start = (bf16[8,4,2048]{2,1,0:T(4,128)(2,1)S(1)}, bf16[8,4,2048]{2,1,0:T(4,128)(2,1)S(1)}, u32[]{:S(2)}, u32[]{:S(2)}) collective-permute-start(bf16[8,4,2048]{2,1,0:T(4,128)(2,1)S(1)} %slice.9), channel_id=1, source_target_pairs={{0,1},{2,3},{4,5},{6,7},{8,9},{10,11},{12,13},{14,15},{16,17},{18,... | collective-permute-start | bytes 393224 | tf_op jit(solution)/shard_map/ppermute | solution.py:20
  6.1 2.4 %copy-start.1 = (bf16[8,128,2048]{2,1,0:T(8,128)(2,1)S(1)}, bf16[8,128,2048]{2,1,0:T(8,128)(2,1)}, u32[]{:S(2)}) copy-start(bf16[8,128,2048]{2,1,0:T(8,128)(2,1)} %volt_ref.1) | copy-start | bytes 12582916
  6.1 2.4 %copy-start.6 = (f32[4,2048]{1,0:T(4,128)S(1)}, f32[4,2048]{1,0:T(4,128)}, u32[]{:S(2)}) copy-start(f32[4,2048]{1,0:T(4,128)} %taps_ref.1) | copy-start | bytes 98308
  13.6 4.4 %collective-permute-start.6 = (bf16[64,16,128]{2,1,0:T(8,128)(2,1)}, bf16[64,16,128]{2,1,0:T(8,128)(2,1)S(1)}, u32[]{:S(2)}, u32[]{:S(2)}) collective-permute-start(bf16[64,16,128]{2,1,0:T(8,128)(2,1)} %get-tuple-element.34), channel_id=1, source_target_pairs={{0,2},{2,0},{1,3},{3,1},{4,6},{6,4},{5,7},{7,5},{8,10},{10,8},{9,1... | collective-permute-start | bytes 786440 | tf_op jit(solution)/shard_map/ppermute | solution.py:25
  15.5 6.4 %copy-start.2 = (bf16[64,16,128]{2,1,0:T(8,128)(2,1)}, bf16[64,16,128]{2,1,0:T(8,128)(2,1)S(1)}, u32[]{:S(2)}) copy-start(bf16[64,16,128]{2,1,0:T(8,128)(2,1)S(1)} %get-tuple-element.23.refs_0_.refs_1_) | copy-start | bytes 786436
  15.5 2.4 %collective-permute-start.1 = (bf16[64,16,128]{2,1,0:T(8,128)(2,1)}, bf16[64,16,128]{2,1,0:T(8,128)(2,1)S(1)}, u32[]{:S(2)}, u32[]{:S(2)}) collective-permute-start(bf16[64,16,128]{2,1,0:T(8,128)(2,1)} %get-tuple-element.25), channel_id=1, source_target_pairs={{0,2},{2,0},{1,3},{3,1},{4,6},{6,4},{5,7},{7,5},{8,10},{10,8},{9,1... | collective-permute-start | bytes 786440 | tf_op jit(solution)/shard_map/ppermute | solution.py:25
  17.9 1.9 %collective-permute-start.5 = (bf16[64,16,128]{2,1,0:T(8,128)(2,1)}, bf16[64,16,128]{2,1,0:T(8,128)(2,1)}, u32[]{:S(2)}, u32[]{:S(2)}) collective-permute-start(bf16[64,16,128]{2,1,0:T(8,128)(2,1)} %get-tuple-element.33), channel_id=1, source_target_pairs={{0,2},{2,0},{1,3},{3,1},{4,6},{6,4},{5,7},{7,5},{8,10},{10,8},{9,1... | collective-permute-start | bytes 786440 | tf_op jit(solution)/shard_map/ppermute | solution.py:25
  18.0 4.0 %copy-start.4 = (bf16[64,16,128]{2,1,0:T(8,128)(2,1)}, bf16[64,16,128]{2,1,0:T(8,128)(2,1)S(1)}, u32[]{:S(2)}) copy-start(bf16[64,16,128]{2,1,0:T(8,128)(2,1)S(1)} %collective-permute-done.1.refs_2_.refs_4_) | copy-start | bytes 786436
  20.9 1.1 copy-start
  22.0 50.2 %all-to-all-start.1 = ((bf16[64,5,16,128]{3,2,1,0:T(8,128)(2,1)}), bf16[64,5,16,128]{3,2,1,0:T(8,128)(2,1)S(1)}, u32[]{:S(2)}, u32[]{:S(2)}) async-start(bf16[64,5,16,128]{3,2,1,0:T(8,128)(2,1)} %copy-done), calls=%async_computation.1 | async-start | bytes 2621440 | tf_op jit(solution)/shard_map/all_to_all | solution.py:274
  38.2 1.6 %collective-permute-start.2 = (bf16[64,16,128]{2,1,0:T(8,128)(2,1)S(1)}, bf16[64,16,128]{2,1,0:T(8,128)(2,1)S(1)}, u32[]{:S(2)}, u32[]{:S(2)}) collective-permute-start(bf16[64,16,128]{2,1,0:T(8,128)(2,1)S(1)} %get-tuple-element.26), channel_id=1, source_target_pairs={{0,2},{2,0},{1,3},{3,1},{4,6},{6,4},{5,7},{7,5},{8,10},{10,8},{9,1... | collective-permute-start | bytes 786440 | tf_op jit(solution)/shard_map/ppermute | solution.py:25
  39.8 1.0 copy-start.3
  40.8 0.9 copy-start.5
  42.4 19.5 %collective-permute-start.3 = (bf16[32,3,16,128]{3,2,1,0:T(8,128)(2,1)S(1)}, bf16[32,3,16,128]{3,2,1,0:T(8,128)(2,1)S(1)}, u32[]{:S(2)}, u32[]{:S(2)}) collective-permute-start(bf16[32,3,16,128]{3,2,1,0:T(8,128)(2,1)S(1)} %get-tuple-element.28), channel_id=1, source_target_pairs={{0,129},{1,128},{128,1},{129,0},{2,131},{3,130},{130,3},{131,2},{4... | collective-permute-start | bytes 1179656 | tf_op jit(solution)/shard_map/ppermute | solution.py:25
  72.2 26.5 %all-to-all-start = ((bf16[32,2,3,16,128]{4,3,2,1,0:T(8,128)(2,1)}), bf16[32,2,3,16,128]{4,3,2,1,0:T(8,128)(2,1)S(1)}, u32[]{:S(2)}, u32[]{:S(2)}) async-start(bf16[32,2,3,16,128]{4,3,2,1,0:T(8,128)(2,1)} %pad_maximum_fusion), calls=%async_computation | async-start | bytes 1572864 | tf_op jit(solution)/shard_map/all_to_all | solution.py:274
  77.8 31.8 %collective-permute-start.7 = (bf16[64,5,16,128]{3,2,1,0:T(8,128)(2,1)S(1)}, bf16[64,5,16,128]{3,2,1,0:T(8,128)(2,1)S(1)}, u32[]{:S(2)}, u32[]{:S(2)}) collective-permute-start(bf16[64,5,16,128]{3,2,1,0:T(8,128)(2,1)S(1)} %all-to-all-done.1.refs_0_.refs_2_), channel_id=1, source_target_pairs={{0,1},{1,0},{2,3},{3,2},{4,5},{5,4},{6,7},{7,6},{8,9},{9,8},{10,11... | collective-permute-start | bytes 3932168 | tf_op jit(solution)/shard_map/ppermute | solution.py:25
  98.7 28.5 %collective-permute-start.4 = (bf16[32,2,2,16,128]{4,3,2,1,0:T(8,128)(2,1)S(1)}, bf16[32,2,2,16,128]{4,3,2,1,0:T(8,128)(2,1)S(1)}, u32[]{:S(2)}, u32[]{:S(2)}) collective-permute-start(bf16[32,2,2,16,128]{4,3,2,1,0:T(8,128)(2,1)S(1)} %slice.12), channel_id=1, source_target_pairs={{0,1},{1,0},{2,3},{3,2},{4,5},{5,4},{6,7},{7,6},{8,9},{9,8},{10,11... | collective-permute-start | bytes 1572872 | tf_op jit(solution)/shard_map/ppermute | solution.py:25
  99.5 24.4 %collective-permute-start.8 = (bf16[32,2,1,16,128]{4,3,2,1,0:T(8,128)(2,1)S(1)}, bf16[32,2,1,16,128]{4,3,2,1,0:T(8,128)(2,1)S(1)}, u32[]{:S(2)}, u32[]{:S(2)}) collective-permute-start(bf16[32,2,1,16,128]{4,3,2,1,0:T(8,128)(2,1)S(1)} %slice.13), channel_id=1, source_target_pairs={{0,1},{1,0},{2,3},{3,2},{4,5},{5,4},{6,7},{7,6},{8,9},{9,8},{10,11... | collective-permute-start | bytes 786440 | tf_op jit(solution)/shard_map/ppermute | solution.py:25

commit v3 on v2

--- a/solution.py
+++ b/solution.py
@@ -11,6 +11,7 @@
 CH = 512
 LANES = 128
 ROWS = 32
+COLUMNS = 512
 MIB = 1024 * 1024
 
 
@@ -136,12 +137,25 @@
 
 def merge_kernel(units, place_ref, *refs):
     arrays = 2 * len({at for at, _ in units})
+    out_ref = refs[arrays]
+    width = out_ref.shape[2] // 2
+    low = place_ref[2] == 0
+    for to, (at, part) in enumerate(units):
+        these = slice(part * width, (part + 1) * width)
+        own = refs[at][:, these].astype(jnp.float32)
+        other = refs[arrays // 2 + at][:, these].astype(jnp.float32)
+        first, second = jnp.where(low, own, other), jnp.where(low, other, own)
+        out_ref[:, to] = jnp.concatenate([first, second], axis=1).astype(jnp.bfloat16)
+
+
+def split_kernel(units, place_ref, *refs):
+    arrays = 2 * len({at for at, _ in units})
     outs = refs[arrays:]
     groups, _, rows, count = outs[0].shape
     width = rows // 2
     low = place_ref[2] == 0
     for side, out_ref in enumerate(outs):
-        first_group = 0 if len(outs) == 1 else jnp.bitwise_xor(place_ref[1], side) * groups
+        first_group = jnp.bitwise_xor(place_ref[1], side) * groups
         for to, (at, part) in enumerate(units):
             these = (pl.ds(first_group, groups), slice(part * width, (part + 1) * width))
             own = refs[at][these].astype(jnp.float32)
@@ -155,96 +169,115 @@
     places = tuple((channels.index(j), part) for j, part in units)
     arrays = [own[j] for j in channels] + [other[j] for j in channels]
     groups, rows, count = arrays[0].shape
+    cost = pl.CostEstimate(flops=0, bytes_accessed=4 * len(units) * groups * rows * count, transcendentals=0)
+    params = pltpu.CompilerParams(vmem_limit_bytes=24 * MIB)
+    if sides == 1:
+        return pl.pallas_call(
+            functools.partial(merge_kernel, places),
+            out_shape=[jax.ShapeDtypeStruct((groups, len(units), rows, count), jnp.bfloat16)],
+            in_specs=[pl.BlockSpec(memory_space=pltpu.SMEM)] + [pl.BlockSpec(memory_space=pltpu.VMEM)] * len(arrays),
+            out_specs=[pl.BlockSpec(memory_space=pltpu.VMEM)],
+            compiler_params=params,
+            cost_estimate=cost,
+            name="merge",
+        )(place, *arrays)
     return pl.pallas_call(
-        functools.partial(merge_kernel, places),
+        functools.partial(split_kernel, places),
         out_shape=[jax.ShapeDtypeStruct((groups // sides, len(units), rows, count), jnp.bfloat16)] * sides,
         in_specs=[pl.BlockSpec(memory_space=pltpu.SMEM)] + [pl.BlockSpec(memory_space=pltpu.VMEM)] * len(arrays),
         out_specs=[pl.BlockSpec(memory_space=pltpu.VMEM)] * sides,
-        compiler_params=pltpu.CompilerParams(vmem_limit_bytes=24 * MIB),
-        cost_estimate=pl.CostEstimate(
-            flops=0, bytes_accessed=4 * len(units) * groups * rows * count, transcendentals=0
-        ),
-        name="merge",
+        compiler_params=params,
+        cost_estimate=cost,
+        name="split",
     )(place, *arrays)
 
 
-def correlate_kernel(scale, place_ref, *refs):
-    out_ref, all_ref, turned_ref = refs[-3:]
-    count = refs[0].shape[-1]
+def correlate_kernel(scale, forms, place_ref, *refs):
+    out_ref, all_ref, rows_ref = refs[-3:]
     inputs = all_ref.shape[0]
-    step = out_ref.shape[2]
-    rows = turned_ref.shape[0]
+    rows = rows_ref.shape[0] // 2
+    step = out_ref.shape[3]
+    half = all_ref.shape[1] // 2
+    count = half // 2
     start = pl.multiple_of(place_ref[0] * rows, rows)
-
-    @pl.when(pl.program_id(0) == 0)
-    def _():
-        for at in range(4):
-            ref = refs[at]
-            sides = 1 if len(ref.shape) == 4 else ref.shape[1]
-            extent = inputs // sides
-            for side in range(sides):
-                slot = at ^ side
-                lanes = slice(slot * count, (slot + 1) * count)
-                if sides == 1:
-                    all_ref[:, lanes] = ref[:, 0].reshape(extent, count)
-                else:
-                    first = jnp.bitwise_xor(place_ref[1], side) * extent
-                    here = pl.ds(pl.multiple_of(first, extent), extent)
-                    all_ref[here, lanes] = ref[:, side, 0].reshape(extent, count)
-        half = 2 * count
-        turned_ref[:, :half] = all_ref[pl.ds(start, rows), half:]
-        turned_ref[:, half:] = -all_ref[pl.ds(start, rows), :half]
-
-    here = pl.multiple_of(pl.program_id(0) * step, step)
-    dot = functools.partial(
-        lax.dot_general, dimension_numbers=(((1,), (1,)), ((), ())), preferred_element_type=jnp.float32
+    column = pl.program_id(1)
+    left = list(refs)
+
+    def gather(parts):
+        for part, (form, sources) in enumerate(parts):
+            slots = [slice((2 * part + slot) * count, (2 * part + slot + 1) * count) for slot in range(2)]
+            if form == "whole":
+                for slot in range(2):
+                    all_ref[:, slots[slot]] = sources[slot][:, 0].reshape(inputs, count)
+                continue
+            extent = inputs // 2
+            for side in range(2):
+                first = jnp.bitwise_xor(place_ref[1], side) * extent
+                here = pl.ds(pl.multiple_of(first, extent), extent)
+                for slot in range(2):
+                    block = sources[0][:, 2 * side + (slot ^ side), 0]
+                    all_ref[here, slots[slot]] = block.reshape(extent, count)
+        rows_ref[:rows] = all_ref[pl.ds(start, rows), :]
+        rows_ref[rows:, :half] = all_ref[pl.ds(start, rows), half:]
+        rows_ref[rows:, half:] = -all_ref[pl.ds(start, rows), :half]
+
+    for at, parts in enumerate(forms):
+        loaded = [(form, [left.pop(0) for _ in range(many)]) for form, many in parts]
+
+        @pl.when((pl.program_id(0) == at) & (column == 0))
+        def _(loaded=loaded):
+            gather(loaded)
+
+    here = pl.multiple_of(column * step, step)
+    both = lax.dot_general(
+        rows_ref[...], all_ref[pl.ds(here, step), :], (((1,), (1,)), ((), ())), preferred_element_type=jnp.float32
     )
-    left = all_ref[pl.ds(start + here, step), :]
-    out_ref[0, 0] = (dot(left, all_ref[...]) * scale).astype(jnp.bfloat16)
-    left = turned_ref[pl.ds(here, step), :]
-    out_ref[1, 0] = (dot(left, all_ref[...]) * scale).astype(jnp.bfloat16)
-
-
-def correlate(place, pieces, result, channel, channels, inputs, parts):
-    count = pieces[0][0].shape[-1]
+    both = (both * scale).astype(jnp.bfloat16)
+    out_ref[0, 0] = both[:rows]
+    out_ref[1, 0] = both[rows:]
+
+
+def correlate(place, pieces, result, first, channels, inputs, parts):
+    count = pieces[0][0][1][0][0].shape[-1]
     rows = inputs // parts
-    step = min(256, rows)
+    step = min(COLUMNS, inputs)
     scale = 1.0 / (parts * count)
     args = [place]
     in_specs = [pl.BlockSpec(memory_space=pltpu.SMEM)]
-    for array, unit in pieces:
-        args.append(array)
-        lead = array.shape[:-3]
-        index = (0,) * len(lead) + (unit, 0, 0)
-        in_specs.append(pl.BlockSpec(lead + (1,) + array.shape[-2:], lambda i, index=index: index))
+    for channel in pieces:
+        for array, unit in (source for _, sources in channel for source in sources):
+            args.append(array)
+            lead = array.shape[:-3]
+            index = (0,) * len(lead) + (unit, 0, 0)
+            in_specs.append(pl.BlockSpec(lead + (1,) + array.shape[-2:], lambda c, i, index=index: index))
     aliases = {}
     if result is not None:
         aliases = {len(args): 0}
         args.append(result)
         in_specs.append(pl.BlockSpec(memory_space=pl.ANY))
+    forms = tuple(tuple((form, len(sources)) for form, sources in channel) for channel in pieces)
     return pl.pallas_call(
-        functools.partial(correlate_kernel, scale),
-        grid=(rows // step,),
+        functools.partial(correlate_kernel, scale, forms),
+        grid=(len(pieces), inputs // step),
         in_specs=in_specs,
-        out_specs=pl.BlockSpec((2, 1, step, inputs), lambda i: (0, channel, i, 0)),
+        out_specs=pl.BlockSpec((2, 1, rows, step), lambda c, i: (0, first + 2 * c, 0, i)),
         out_shape=jax.ShapeDtypeStruct((2, channels, rows, inputs), jnp.bfloat16),
         scratch_shapes=[
             pltpu.VMEM((inputs, 2 * parts * count), jnp.bfloat16),
-            pltpu.VMEM((rows, 2 * parts * count), jnp.bfloat16),
+            pltpu.VMEM((2 * rows, 2 * parts * count), jnp.bfloat16),
         ],
         input_output_aliases=aliases,
         compiler_params=pltpu.CompilerParams(vmem_limit_bytes=24 * MIB),
         cost_estimate=pl.CostEstimate(
-            flops=8 * rows * inputs * parts * count, bytes_accessed=4 * rows * inputs, transcendentals=0
+            flops=8 * len(pieces) * rows * inputs * parts * count,
+            bytes_accessed=4 * len(pieces) * rows * inputs, transcendentals=0,
         ),
         name="correlate",
     )(*args)
 
 
-CHUNKS = (((0, 0), (0, 1), (2, 0), (2, 1), (1, 0)), ((1, 1), (3, 0), (3, 1)))
-SPLIT = 1
-
-
+CHUNKS = (((0, 0), (0, 1), (2, 0), (2, 1), (1, 0), (1, 1)), ((3, 0), (3, 1)))
+SPLIT = 4
 def body(voltages, taps):
     width, count, npoints = voltages.shape
     parts = lax.axis_size("tm")
@@ -265,25 +298,23 @@
             other[j] = swapped(send, "core")
         if n == 0:
             (block,) = merge(place, units, own, other, 1)
-            axes = ("yh", "x", "chip")
+            block = lax.all_to_all(block, ("yh", "x", "chip"), split_axis=0, concat_axis=0, tiled=True)
+            for first, last in ((0, SPLIT), (SPLIT, len(units))):
+                far = swapped(block[:, first:last], "tm")
+                for at in range(first, last):
+                    arrived[units[at]] = ("whole", [(block, at), (far, at - first)])
         else:
             here, across = merge(place, units, own, other, 2)
             across = swapped(across, ("yh", "tm"))
-            block = jnp.stack([here, across], axis=1)
-            axes = ("x", "chip")
-        block = lax.all_to_all(block, axes, split_axis=0, concat_axis=0, tiled=True)
-        split = SPLIT if n else len(units)
-        for first, last in ((0, split), (split, len(units))):
-            if first == last:
-                continue
-            far = block if n == 0 else block[:, :, first:last]
-            far = swapped(far, "tm")
-            for at in range(first, last):
-                arrived[units[at]] = [(block, at), (far, at - first)]
+            block = jnp.stack([here, swapped(here, "tm"), across, swapped(across, "tm")], axis=1)
+            block = lax.all_to_all(block, ("x", "chip"), split_axis=0, concat_axis=0, tiled=True)
+            for at, unit in enumerate(units):
+                arrived[unit] = ("sides", [(block, at)])
     result = None
     inputs = groups * cores * width
-    for j in (0, 2, 1, 3):
-        result = correlate(place, arrived[j, 0] + arrived[j, 1], result, j, per_group, inputs, parts)
+    for together in ((0, 2), (3,), (1,)):
+        pieces = [(arrived[j, 0], arrived[j, 1]) for j in together]
+        result = correlate(place, pieces, result, together[0], per_group, inputs, parts)
     return result
 
 

time: 131 us -> 121 us (0.924)
  waiting for transfers between devices: 65.5 us -> 58.9 us
  Pallas kernels: 25 us -> 22.5 us
  other arithmetic: 4.7 us -> 3 us
  local copies, waits for them, and re-layouts: 5.27 us -> 6.63 us
    all_to_all x2, waiting for transfers between devices: 29.3 us -> 7.62 us  [the longest x1 7.61 us: body(): lax.all_to_all(block, ('yh', 'x', 'chip'), split_axis=0, concat_axis=0, t...]
    ppermute x8 -> x9, waiting for transfers between devices: 36.2 us -> 51 us  [swapped(): return lax.ppermute(block, axis, [(i, size - 1 - i) for i in range(size)])]
    pallas_call x4, Pallas kernels: 6.81 us -> 4.68 us  [spectra(): pl.pallas_call(functools.partial(spectra_kernel, width), out_shape=[jax.S...]
    ppermute x8 -> x9, starting transfers between devices: 6.67 us -> 6.2 us  [swapped(): return lax.ppermute(block, axis, [(i, size - 1 - i) for i in range(size)])]
    unnamed x16 -> x10, local copies, waits for them, and re-layouts: 3.81 us -> 4.11 us
  transfers between devices with their start and end apart: 11 -> 12, of which waited for: 7 -> 9; matrix products, arithmetic and copies ran while one was open for 4% -> 4% of each run, Pallas kernels for 12% -> 10%
where the time goes in v3:
time: 121 us
  waiting for transfers between devices  58.9 us (49%)
  starting transfers between devices  29.2 us (24%)
  Pallas kernels  22.5 us (19%)
  local copies, waits for them, and re-layouts  6.63 us (5%)
  other arithmetic  3 us (2%)
    ppermute x9, waiting for transfers between devices, swapped(): return lax.ppermute(block, axis, [(i, size - 1 - i) for i in range(size)])  51 us
    all_to_all x1, starting transfers between devices, body(): lax.all_to_all(block, ('yh', 'x', 'chip'), split_axis=0, concat_axis=0, t...  13.9 us
    pallas_call x3, Pallas kernels, correlate(): pl.pallas_call(functools.partial(correlate_kernel, scale, forms), grid=(l...  11.9 us
    all_to_all x1, waiting for transfers between devices, body(): lax.all_to_all(block, ('yh', 'x', 'chip'), split_axis=0, concat_axis=0, t...  7.61 us
    ppermute x9, starting transfers between devices, swapped(): return lax.ppermute(block, axis, [(i, size - 1 - i) for i in range(size)])  6.2 us
    all_to_all x1, starting transfers between devices, body(): lax.all_to_all(block, ('x', 'chip'), split_axis=0, concat_axis=0, tiled=T...  5.62 us
    pallas_call x4, Pallas kernels, spectra(): pl.pallas_call(functools.partial(spectra_kernel, width), out_shape=[jax.S...  4.68 us
    unnamed x10, local copies, waits for them, and re-layouts  4.11 us
  transfers between devices with their start and end apart: 12, of which 9 were waited for; matrix products, arithmetic and copies ran while one was open for 4% of the time, Pallas kernels for 10%

profile of v3, /device:TPU:38, one launch (start us, length us, event | category | flops | bytes accessed | tf_op | source)
XLA Modules:
  0.0 120.6 jit_solution(14879839758877023777)
XLA Ops:
  0.0 1.0 slice.9
  1.0 3.5 %collective-permute-start = (bf16[8,4,2048]{2,1,0:T(4,128)(2,1)S(1)}, bf16[8,4,2048]{2,1,0:T(4,128)(2,1)S(1)}, u32[]{:S(2)}, u32[]{:S(2)}) collective-permute-start(bf16[8,4,2048]{2,1,0:T(4,128)(2,1)S(1)} %slice.9), channel_id=1, source_target_pairs={{0,1},{2,3},{4,5},{6,7},{8,9},{10,11},{12,13},{14,15},{16,17},{18,... | collective-permute-start | bytes 393224 | tf_op jit(solution)/shard_map/ppermute | solution.py:21
  4.8 1.1 fusion.6
  7.3 1.0 copy-done.2
  8.3 3.3 %filter_bank.1 = (bf16[1024,512]{1,0:T(8,128)(2,1)S(1)}, bf16[1024,512]{1,0:T(8,128)(2,1)S(1)}, bf16[1024,1024]{1,0:T(8,128)(2,1)S(1)}) custom-call(bf16[8,128,2048]{2,1,0:T(8,128)(2,1)S(1)} %copy-done.2, bf16[8,4,2048]{2,1,0:T(4,128)(2,1)S(1)} %collective-permute-done.hist_ref, f32[4,2048]{1,0:T(4,128)S(1)} %copy-done.3), custom_call_target="tpu_custom_call" | custom-call | flops 41943040 | bytes 8388608 | tf_op jit(solution)/shard_map/filter_bank/pallas_call | solution.py:89
  11.6 1.3 %spectra.5 = (bf16[64,16,128]{2,1,0:T(8,128)(2,1)S(1)}, bf16[64,16,128]{2,1,0:T(8,128)(2,1)S(1)}) custom-call(bf16[256,1024]{1,0:T(8,128)(2,1)S(1)} %pad_maximum_fusion.1.table_ref, bf16[1024,1024]{1,0:T(8,128)(2,1)S(1)} %get-tuple-element.24.filt_ref), custom_call_target="tpu_custom_call" | custom-call | flops 536870912 | bytes 2097152 | tf_op jit(solution)/shard_map/spectra/pallas_call | solution.py:124
  12.9 1.3 %copy-done = bf16[1024,1024]{1,0:T(8,128)(2,1)} copy-done((bf16[1024,1024]{1,0:T(8,128)(2,1)}, bf16[1024,1024]{1,0:T(8,128)(2,1)S(1)}, u32[]{:S(2)}) %copy-start) | copy-done | bytes 2097176
  14.2 1.1 spectra.6
  15.3 0.6 collective-permute-start.3
  15.9 1.1 spectra.4
  17.2 1.4 %collective-permute-done.1.refs_3_ = bf16[64,16,128]{2,1,0:T(8,128)(2,1)S(1)} collective-permute-done((bf16[64,16,128]{2,1,0:T(8,128)(2,1)S(1)}, bf16[64,16,128]{2,1,0:T(8,128)(2,1)S(1)}, u32[]{:S(2)}, u32[]{:S(2)}) %collective-permute-start.1) | collective-permute-done | bytes 262176 | tf_op jit(solution)/shard_map/ppermute | solution.py:26
  18.6 2.0 %merge.1 = bf16[64,6,16,128]{3,2,1,0:T(8,128)(2,1)} custom-call(s32[3]{0:T(128)S(1)} %pad_add_fusion.place_ref, bf16[64,16,128]{2,1,0:T(8,128)(2,1)S(1)} %get-tuple-element.23.refs_0_, bf16[64,16,128]{2,1,0:T(8,128)(2,1)S(1)} %get-tuple-element.25.refs_1_, bf16[64,16,128]{2,1,0:T(8,128)(2,1)S(1)} %get-tuple-element.27.refs_2_, ...), custom_call_target="tpu_custom_call" | custom-call | bytes 3145728 | tf_op jit(solution)/shard_map/merge/pallas_call | solution.py:175
  20.6 13.9 %all-to-all-start = ((bf16[64,6,16,128]{3,2,1,0:T(8,128)(2,1)}), bf16[64,6,16,128]{3,2,1,0:T(8,128)(2,1)S(1)}, u32[]{:S(2)}, u32[]{:S(2)}) async-start(bf16[64,6,16,128]{3,2,1,0:T(8,128)(2,1)} %merge.1), calls=%async_computation | async-start | bytes 3145728 | tf_op jit(solution)/shard_map/all_to_all | solution.py:301
  34.6 1.6 %copy-done.1 = bf16[1024,1024]{1,0:T(8,128)(2,1)S(1)} copy-done((bf16[1024,1024]{1,0:T(8,128)(2,1)S(1)}, bf16[1024,1024]{1,0:T(8,128)(2,1)}, u32[]{:S(2)}) %copy-start.1) | copy-done | bytes 2097176
  36.2 1.2 %spectra.7 = (bf16[64,16,128]{2,1,0:T(8,128)(2,1)S(1)}, bf16[64,16,128]{2,1,0:T(8,128)(2,1)S(1)}) custom-call(bf16[256,1024]{1,0:T(8,128)(2,1)S(1)} %pad_maximum_fusion.2.table_ref, bf16[1024,1024]{1,0:T(8,128)(2,1)S(1)} %copy-done.1), custom_call_target="tpu_custom_call" | custom-call | flops 536870912 | bytes 2097152 | tf_op jit(solution)/shard_map/spectra/pallas_call | solution.py:124
  37.5 1.5 %collective-permute-done.5.refs_1_ = bf16[64,16,128]{2,1,0:T(8,128)(2,1)S(1)} collective-permute-done((bf16[64,16,128]{2,1,0:T(8,128)(2,1)S(1)}, bf16[64,16,128]{2,1,0:T(8,128)(2,1)S(1)}, u32[]{:S(2)}, u32[]{:S(2)}) %collective-permute-start.5) | collective-permute-done | bytes 262176 | tf_op jit(solution)/shard_map/ppermute | solution.py:26
  39.0 0.6 split.1
  39.7 3.3 %collective-permute-start.7 = (bf16[32,2,16,128]{3,2,1,0:T(8,128)(2,1)S(1)}, bf16[32,2,16,128]{3,2,1,0:T(8,128)(2,1)S(1)}, u32[]{:S(2)}, u32[]{:S(2)}) collective-permute-start(bf16[32,2,16,128]{3,2,1,0:T(8,128)(2,1)S(1)} %get-tuple-element.34), channel_id=1, source_target_pairs={{0,129},{1,128},{128,1},{129,0},{2,131},{3,130},{130,3},{131,2},{4... | collective-permute-start | bytes 786440 | tf_op jit(solution)/shard_map/ppermute | solution.py:26
  43.0 9.6 %collective-permute-done.7 = bf16[32,2,16,128]{3,2,1,0:T(8,128)(2,1)S(1)} collective-permute-done((bf16[32,2,16,128]{3,2,1,0:T(8,128)(2,1)S(1)}, bf16[32,2,16,128]{3,2,1,0:T(8,128)(2,1)S(1)}, u32[]{:S(2)}, u32[]{:S(2)}) %collective-permute-start.7) | collective-permute-done | bytes 262176 | tf_op jit(solution)/shard_map/ppermute | solution.py:26
  52.6 1.7 %collective-permute-done.6 = bf16[32,2,16,128]{3,2,1,0:T(8,128)(2,1)S(1)} collective-permute-done((bf16[32,2,16,128]{3,2,1,0:T(8,128)(2,1)S(1)}, bf16[32,2,16,128]{3,2,1,0:T(8,128)(2,1)S(1)}, u32[]{:S(2)}, u32[]{:S(2)}) %collective-permute-start.6) | collective-permute-done | bytes 262176 | tf_op jit(solution)/shard_map/ppermute | solution.py:26
  54.3 13.4 %collective-permute-done.8 = bf16[32,2,16,128]{3,2,1,0:T(8,128)(2,1)S(1)} collective-permute-done((bf16[32,2,16,128]{3,2,1,0:T(8,128)(2,1)S(1)}, bf16[32,2,16,128]{3,2,1,0:T(8,128)(2,1)S(1)}, u32[]{:S(2)}, u32[]{:S(2)}) %collective-permute-start.8) | collective-permute-done | bytes 262176 | tf_op jit(solution)/shard_map/ppermute | solution.py:26
  67.7 1.1 pad_maximum_fusion
  68.8 7.6 %all-to-all-done.refs_0_.refs_2_.refs_4_.refs_6_ = bf16[64,6,16,128]{3,2,1,0:T(8,128)(2,1)S(1)} async-done(((bf16[64,6,16,128]{3,2,1,0:T(8,128)(2,1)}), bf16[64,6,16,128]{3,2,1,0:T(8,128)(2,1)S(1)}, u32[]{:S(2)}, u32[]{:S(2)}) %all-to-all-start) | async-done | bytes 1572896 | tf_op jit(solution)/shard_map/all_to_all | solution.py:301
  76.4 5.6 %all-to-all-start.1 = ((bf16[32,4,2,16,128]{4,3,2,1,0:T(8,128)(2,1)}), bf16[32,4,2,16,128]{4,3,2,1,0:T(8,128)(2,1)S(1)}, u32[]{:S(2)}, u32[]{:S(2)}) async-start(bf16[32,4,2,16,128]{4,3,2,1,0:T(8,128)(2,1)} %pad_maximum_fusion), calls=%async_computation.1 | async-start | bytes 2097152 | tf_op jit(solution)/shard_map/all_to_all | solution.py:310
  82.0 0.3 slice.13
  82.3 1.0 collective-permute-start.9
  83.3 0.9 slice.12
  84.1 1.2 collective-permute-start.4
  85.3 23.2 %collective-permute-done.9.refs_1_.refs_3_.refs_5_.refs_7_ = bf16[64,4,16,128]{3,2,1,0:T(8,128)(2,1)S(1)} collective-permute-done((bf16[64,4,16,128]{3,2,1,0:T(8,128)(2,1)S(1)}, bf16[64,4,16,128]{3,2,1,0:T(8,128)(2,1)S(1)}, u32[]{:S(2)}, u32[]{:S(2)}) %collective-permute-start.9) | collective-permute-done | bytes 1048608 | tf_op jit(solution)/shard_map/ppermute | solution.py:26
  108.5 5.3 %correlate.3.refs_2_ = bf16[2,4,512,1024]{3,2,1,0:T(8,128)(2,1)} custom-call(s32[3]{0:T(128)S(1)} %pad_add_fusion.place_ref, bf16[64,6,16,128]{3,2,1,0:T(8,128)(2,1)S(1)} %all-to-all-done.refs_0_.refs_2_.refs_4_.refs_6_, bf16[64,4,16,128]{3,2,1,0:T(8,128)(2,1)S(1)} %collective-permute-done.9.refs_1_.refs_3_.refs_5_.refs_7_, ...), custom_call_target="tpu_custom_call" | custom-call | flops 2147483648 | bytes 4194304 | tf_op jit(solution)/shard_map/correlate/pallas_call | solution.py:259
  113.8 3.3 %correlate.4.refs_4_ = bf16[2,4,512,1024]{3,2,1,0:T(8,128)(2,1)} custom-call(s32[3]{0:T(128)S(1)} %pad_add_fusion.place_ref, bf16[32,4,2,16,128]{4,3,2,1,0:T(8,128)(2,1)S(1)} %all-to-all-done.1.refs_0_.refs_1_, bf16[32,4,2,16,128]{4,3,2,1,0:T(8,128)(2,1)S(1)} %all-to-all-done.1.refs_0_.refs_1_, ...), custom_call_target="tpu_custom_call", output_to_operand_aliasing={{}: (3, {})} | custom-call | flops 1073741824 | bytes 2097152 | tf_op jit(solution)/shard_map/correlate/pallas_call | solution.py:259
  117.3 3.3 %correlate.5 = bf16[2,4,512,1024]{3,2,1,0:T(8,128)(2,1)} custom-call(s32[3]{0:T(128)S(1)} %pad_add_fusion.place_ref, bf16[64,6,16,128]{3,2,1,0:T(8,128)(2,1)S(1)} %all-to-all-done.refs_0_.refs_2_.refs_4_.refs_6_, bf16[64,2,16,128]{3,2,1,0:T(8,128)(2,1)S(1)} %collective-permute-done.4.refs_1_.refs_3_, ...), custom_call_target="tpu_custom_call", output_to_operand_aliasing={{}: (5, {})} | custom-call | flops 1073741824 | bytes 2097152 | tf_op jit(solution)/shard_map/correlate/pallas_call | solution.py:259
  (31 shorter events, 2.0 us)
Async XLA Ops:
  1.0 6.2 %collective-permute-start = (bf16[8,4,2048]{2,1,0:T(4,128)(2,1)S(1)}, bf16[8,4,2048]{2,1,0:T(4,128)(2,1)S(1)}, u32[]{:S(2)}, u32[]{:S(2)}) collective-permute-start(bf16[8,4,2048]{2,1,0:T(4,128)(2,1)S(1)} %slice.9), channel_id=1, source_target_pairs={{0,1},{2,3},{4,5},{6,7},{8,9},{10,11},{12,13},{14,15},{16,17},{18,... | collective-permute-start | bytes 393224 | tf_op jit(solution)/shard_map/ppermute | solution.py:21
  6.1 2.2 %copy-start.2 = (bf16[8,128,2048]{2,1,0:T(8,128)(2,1)S(1)}, bf16[8,128,2048]{2,1,0:T(8,128)(2,1)}, u32[]{:S(2)}) copy-start(bf16[8,128,2048]{2,1,0:T(8,128)(2,1)} %volt_ref.1) | copy-start | bytes 12582916
  6.1 2.2 %copy-start.3 = (f32[4,2048]{1,0:T(4,128)S(1)}, f32[4,2048]{1,0:T(4,128)}, u32[]{:S(2)}) copy-start(f32[4,2048]{1,0:T(4,128)} %taps_ref.1) | copy-start | bytes 98308
  12.9 1.3 %copy-start = (bf16[1024,1024]{1,0:T(8,128)(2,1)}, bf16[1024,1024]{1,0:T(8,128)(2,1)S(1)}, u32[]{:S(2)}) copy-start(bf16[1024,1024]{1,0:T(8,128)(2,1)S(1)} %get-tuple-element.24.filt_ref) | copy-start | bytes 6291460
  14.2 3.0 %collective-permute-start.2 = (bf16[64,16,128]{2,1,0:T(8,128)(2,1)S(1)}, bf16[64,16,128]{2,1,0:T(8,128)(2,1)S(1)}, u32[]{:S(2)}, u32[]{:S(2)}) collective-permute-start(bf16[64,16,128]{2,1,0:T(8,128)(2,1)S(1)} %get-tuple-element.29), channel_id=1, source_target_pairs={{0,2},{2,0},{1,3},{3,1},{4,6},{6,4},{5,7},{7,5},{8,10},{10,8},{9,1... | collective-permute-start | bytes 786440 | tf_op jit(solution)/shard_map/ppermute | solution.py:26
  15.3 1.9 %collective-permute-start.3 = (bf16[64,16,128]{2,1,0:T(8,128)(2,1)S(1)}, bf16[64,16,128]{2,1,0:T(8,128)(2,1)S(1)}, u32[]{:S(2)}, u32[]{:S(2)}) collective-permute-start(bf16[64,16,128]{2,1,0:T(8,128)(2,1)S(1)} %get-tuple-element.30), channel_id=1, source_target_pairs={{0,2},{2,0},{1,3},{3,1},{4,6},{6,4},{5,7},{7,5},{8,10},{10,8},{9,1... | collective-permute-start | bytes 786440 | tf_op jit(solution)/shard_map/ppermute | solution.py:26
  17.0 1.6 %collective-permute-start.1 = (bf16[64,16,128]{2,1,0:T(8,128)(2,1)S(1)}, bf16[64,16,128]{2,1,0:T(8,128)(2,1)S(1)}, u32[]{:S(2)}, u32[]{:S(2)}) collective-permute-start(bf16[64,16,128]{2,1,0:T(8,128)(2,1)S(1)} %get-tuple-element.28), channel_id=1, source_target_pairs={{0,2},{2,0},{1,3},{3,1},{4,6},{6,4},{5,7},{7,5},{8,10},{10,8},{9,1... | collective-permute-start | bytes 786440 | tf_op jit(solution)/shard_map/ppermute | solution.py:26
  20.6 55.8 %all-to-all-start = ((bf16[64,6,16,128]{3,2,1,0:T(8,128)(2,1)}), bf16[64,6,16,128]{3,2,1,0:T(8,128)(2,1)S(1)}, u32[]{:S(2)}, u32[]{:S(2)}) async-start(bf16[64,6,16,128]{3,2,1,0:T(8,128)(2,1)} %merge.1), calls=%async_computation | async-start | bytes 3145728 | tf_op jit(solution)/shard_map/all_to_all | solution.py:301
  34.6 1.6 %copy-start.1 = (bf16[1024,1024]{1,0:T(8,128)(2,1)S(1)}, bf16[1024,1024]{1,0:T(8,128)(2,1)}, u32[]{:S(2)}) copy-start(bf16[1024,1024]{1,0:T(8,128)(2,1)} %copy-done) | copy-start | bytes 6291460
  37.4 1.6 %collective-permute-start.5 = (bf16[64,16,128]{2,1,0:T(8,128)(2,1)S(1)}, bf16[64,16,128]{2,1,0:T(8,128)(2,1)S(1)}, u32[]{:S(2)}, u32[]{:S(2)}) collective-permute-start(bf16[64,16,128]{2,1,0:T(8,128)(2,1)S(1)} %get-tuple-element.32), channel_id=1, source_target_pairs={{0,2},{2,0},{1,3},{3,1},{4,6},{6,4},{5,7},{7,5},{8,10},{10,8},{9,1... | collective-permute-start | bytes 786440 | tf_op jit(solution)/shard_map/ppermute | solution.py:26
  39.7 12.9 %collective-permute-start.7 = (bf16[32,2,16,128]{3,2,1,0:T(8,128)(2,1)S(1)}, bf16[32,2,16,128]{3,2,1,0:T(8,128)(2,1)S(1)}, u32[]{:S(2)}, u32[]{:S(2)}) collective-permute-start(bf16[32,2,16,128]{3,2,1,0:T(8,128)(2,1)S(1)} %get-tuple-element.34), channel_id=1, source_target_pairs={{0,129},{1,128},{128,1},{129,0},{2,131},{3,130},{130,3},{131,2},{4... | collective-permute-start | bytes 786440 | tf_op jit(solution)/shard_map/ppermute | solution.py:26
  43.0 11.4 %collective-permute-start.6 = (bf16[32,2,16,128]{3,2,1,0:T(8,128)(2,1)S(1)}, bf16[32,2,16,128]{3,2,1,0:T(8,128)(2,1)S(1)}, u32[]{:S(2)}, u32[]{:S(2)}) collective-permute-start(bf16[32,2,16,128]{3,2,1,0:T(8,128)(2,1)S(1)} %get-tuple-element.33), channel_id=1, source_target_pairs={{0,1},{1,0},{2,3},{3,2},{4,5},{5,4},{6,7},{7,6},{8,9},{9,8},{10,11... | collective-permute-start | bytes 786440 | tf_op jit(solution)/shard_map/ppermute | solution.py:26
  52.6 15.1 %collective-permute-start.8 = (bf16[32,2,16,128]{3,2,1,0:T(8,128)(2,1)S(1)}, bf16[32,2,16,128]{3,2,1,0:T(8,128)(2,1)S(1)}, u32[]{:S(2)}, u32[]{:S(2)}) collective-permute-start(bf16[32,2,16,128]{3,2,1,0:T(8,128)(2,1)S(1)} %collective-permute-done.7), channel_id=1, source_target_pairs={{0,1},{1,0},{2,3},{3,2},{4,5},{5,4},{6,7},{7,6},{8,9},{9,8},{10,11... | collective-permute-start | bytes 786440 | tf_op jit(solution)/shard_map/ppermute | solution.py:26
  76.4 37.4 %all-to-all-start.1 = ((bf16[32,4,2,16,128]{4,3,2,1,0:T(8,128)(2,1)}), bf16[32,4,2,16,128]{4,3,2,1,0:T(8,128)(2,1)S(1)}, u32[]{:S(2)}, u32[]{:S(2)}) async-start(bf16[32,4,2,16,128]{4,3,2,1,0:T(8,128)(2,1)} %pad_maximum_fusion), calls=%async_computation.1 | async-start | bytes 2097152 | tf_op jit(solution)/shard_map/all_to_all | solution.py:310
  82.3 26.2 %collective-permute-start.9 = (bf16[64,4,16,128]{3,2,1,0:T(8,128)(2,1)S(1)}, bf16[64,4,16,128]{3,2,1,0:T(8,128)(2,1)S(1)}, u32[]{:S(2)}, u32[]{:S(2)}) collective-permute-start(bf16[64,4,16,128]{3,2,1,0:T(8,128)(2,1)S(1)} %slice.13), channel_id=1, source_target_pairs={{0,1},{1,0},{2,3},{3,2},{4,5},{5,4},{6,7},{7,6},{8,9},{9,8},{10,11... | collective-permute-start | bytes 3145736 | tf_op jit(solution)/shard_map/ppermute | solution.py:26
  84.1 33.1 %collective-permute-start.4 = (bf16[64,2,16,128]{3,2,1,0:T(8,128)(2,1)}, bf16[64,2,16,128]{3,2,1,0:T(8,128)(2,1)S(1)}, u32[]{:S(2)}, u32[]{:S(2)}) collective-permute-start(bf16[64,2,16,128]{3,2,1,0:T(8,128)(2,1)} %slice.12), channel_id=1, source_target_pairs={{0,1},{1,0},{2,3},{3,2},{4,5},{5,4},{6,7},{7,6},{8,9},{9,8},{10,11... | collective-permute-start | bytes 1572872 | tf_op jit(solution)/shard_map/ppermute | solution.py:26

commit v4 on v3

--- a/solution.py
+++ b/solution.py
@@ -12,6 +12,7 @@
 LANES = 128
 ROWS = 32
 COLUMNS = 512
+WEIGHT = 4
 MIB = 1024 * 1024
 
 
@@ -46,9 +47,12 @@
     return out
 
 
-def filter_kernel(volt_ref, hist_ref, taps_ref, sum_ref, alt_ref, diff_ref, wide_ref):
+def filter_kernel(source_ref, hist_ref, taps_ref, sum_ref, alt_ref, diff_ref, volt_ref, wide_ref, sems):
     ntaps = taps_ref.shape[0]
     width, count, _ = volt_ref.shape
+    loads = [pltpu.make_async_copy(source_ref.at[i], volt_ref.at[i], sems.at[i]) for i in range(width)]
+    for load in loads:
+        load.start()
     quarter = sum_ref.shape[1]
     nhist = hist_ref.shape[1]
     pad = 8
@@ -56,6 +60,7 @@
 
     @pl.loop(0, width)
     def _(i):
+        pltpu.make_async_copy(source_ref.at[i], volt_ref.at[i], sems.at[i]).wait()
         for start in range(0, quarter, LANES):
             places = [slice(start + slot * quarter, start + slot * quarter + LANES) for slot in range(4)]
             for slot, lanes in enumerate(places):
@@ -88,10 +93,14 @@
     depths = (quarter, quarter, half)
     return pl.pallas_call(
         filter_kernel,
-        in_specs=[pl.BlockSpec(memory_space=pltpu.VMEM)] * 3,
+        in_specs=[pl.BlockSpec(memory_space=pltpu.HBM)] + [pl.BlockSpec(memory_space=pltpu.VMEM)] * 2,
         out_specs=[pl.BlockSpec(memory_space=pltpu.VMEM)] * 3,
         out_shape=[jax.ShapeDtypeStruct((rows, d), jnp.bfloat16) for d in depths],
-        scratch_shapes=[pltpu.VMEM((4, 8 + count, LANES), jnp.float32)],
+        scratch_shapes=[
+            pltpu.VMEM(voltages.shape, voltages.dtype),
+            pltpu.VMEM((4, 8 + count, LANES), jnp.float32),
+            pltpu.SemaphoreType.DMA((width,)),
+        ],
         compiler_params=pltpu.CompilerParams(vmem_limit_bytes=24 * MIB),
         cost_estimate=pl.CostEstimate(flops=20 * rows * npoints, bytes_accessed=4 * rows * npoints, transcendentals=0),
         name="filter_bank",
@@ -137,7 +146,7 @@
 
 def merge_kernel(units, place_ref, *refs):
     arrays = 2 * len({at for at, _ in units})
-    out_ref = refs[arrays]
+    out_ref = refs[-1]
     width = out_ref.shape[2] // 2
     low = place_ref[2] == 0
     for to, (at, part) in enumerate(units):
@@ -164,28 +173,45 @@
             out_ref[:, to] = jnp.concatenate([first, second], axis=1).astype(jnp.bfloat16)
 
 
-def merge(place, units, own, other, sides):
+def merge_into(place, units, own, other, result, first, total):
+    channels = sorted({j for j, _ in units})
+    places = tuple((channels.index(j), part) for j, part in units)
+    arrays = [own[j] for j in channels] + [other[j] for j in channels]
+    groups, rows, count = arrays[0].shape
+    whole = pl.BlockSpec((groups, rows, count), lambda i: (0, 0, 0))
+    in_specs = [pl.BlockSpec(memory_space=pltpu.SMEM)] + [whole] * len(arrays)
+    args, aliases = [place] + arrays, {}
+    if result is not None:
+        aliases = {len(args): 0}
+        args.append(result)
+        in_specs.append(pl.BlockSpec(memory_space=pl.ANY))
+    return pl.pallas_call(
+        functools.partial(merge_kernel, places),
+        grid=(1,),
+        out_shape=jax.ShapeDtypeStruct((groups, total, rows, count), jnp.bfloat16),
+        in_specs=in_specs,
+        out_specs=pl.BlockSpec((groups, len(units), rows, count), lambda i: (0, first // len(units), 0, 0)),
+        input_output_aliases=aliases,
+        compiler_params=pltpu.CompilerParams(vmem_limit_bytes=24 * MIB),
+        cost_estimate=pl.CostEstimate(
+            flops=0, bytes_accessed=4 * len(units) * groups * rows * count, transcendentals=0
+        ),
+        name="merge",
+    )(*args)
+
+
+def split(place, units, own, other):
     channels = sorted({j for j, _ in units})
     places = tuple((channels.index(j), part) for j, part in units)
     arrays = [own[j] for j in channels] + [other[j] for j in channels]
     groups, rows, count = arrays[0].shape
     cost = pl.CostEstimate(flops=0, bytes_accessed=4 * len(units) * groups * rows * count, transcendentals=0)
     params = pltpu.CompilerParams(vmem_limit_bytes=24 * MIB)
-    if sides == 1:
-        return pl.pallas_call(
-            functools.partial(merge_kernel, places),
-            out_shape=[jax.ShapeDtypeStruct((groups, len(units), rows, count), jnp.bfloat16)],
-            in_specs=[pl.BlockSpec(memory_space=pltpu.SMEM)] + [pl.BlockSpec(memory_space=pltpu.VMEM)] * len(arrays),
-            out_specs=[pl.BlockSpec(memory_space=pltpu.VMEM)],
-            compiler_params=params,
-            cost_estimate=cost,
-            name="merge",
-        )(place, *arrays)
     return pl.pallas_call(
         functools.partial(split_kernel, places),
-        out_shape=[jax.ShapeDtypeStruct((groups // sides, len(units), rows, count), jnp.bfloat16)] * sides,
+        out_shape=[jax.ShapeDtypeStruct((groups // 2, len(units), rows, count), jnp.bfloat16)] * 2,
         in_specs=[pl.BlockSpec(memory_space=pltpu.SMEM)] + [pl.BlockSpec(memory_space=pltpu.VMEM)] * len(arrays),
-        out_specs=[pl.BlockSpec(memory_space=pltpu.VMEM)] * sides,
+        out_specs=[pl.BlockSpec(memory_space=pltpu.VMEM)] * 2,
         compiler_params=params,
         cost_estimate=cost,
         name="split",
@@ -269,7 +295,7 @@
         input_output_aliases=aliases,
         compiler_params=pltpu.CompilerParams(vmem_limit_bytes=24 * MIB),
         cost_estimate=pl.CostEstimate(
-            flops=8 * len(pieces) * rows * inputs * parts * count,
+            flops=WEIGHT * 8 * len(pieces) * rows * inputs * parts * count,
             bytes_accessed=4 * len(pieces) * rows * inputs, transcendentals=0,
         ),
         name="correlate",
@@ -297,14 +323,15 @@
             own[j], send = spectra(table[j], sources[j], width, groups)
             other[j] = swapped(send, "core")
         if n == 0:
-            (block,) = merge(place, units, own, other, 1)
+            block = merge_into(place, units[:SPLIT], own, other, None, 0, len(units))
+            block = merge_into(place, units[SPLIT:], own, other, block, SPLIT, len(units))
             block = lax.all_to_all(block, ("yh", "x", "chip"), split_axis=0, concat_axis=0, tiled=True)
             for first, last in ((0, SPLIT), (SPLIT, len(units))):
                 far = swapped(block[:, first:last], "tm")
                 for at in range(first, last):
                     arrived[units[at]] = ("whole", [(block, at), (far, at - first)])
         else:
-            here, across = merge(place, units, own, other, 2)
+            here, across = split(place, units, own, other)
             across = swapped(across, ("yh", "tm"))
             block = jnp.stack([here, swapped(here, "tm"), across, swapped(across, "tm")], axis=1)
             block = lax.all_to_all(block, ("x", "chip"), split_axis=0, concat_axis=0, tiled=True)
@@ -312,7 +339,7 @@
                 arrived[unit] = ("sides", [(block, at)])
     result = None
     inputs = groups * cores * width
-    for together in ((0, 2), (3,), (1,)):
+    for together in ((0, 2), (1,), (3,)):
         pieces = [(arrived[j, 0], arrived[j, 1]) for j in together]
         result = correlate(place, pieces, result, together[0], per_group, inputs, parts)
     return result

time: 121 us -> 119 us (0.983)
  waiting for transfers between devices: 58.9 us -> 55.7 us
  Pallas kernels: 22.5 us -> 24.9 us
    ppermute x9, waiting for transfers between devices: 51 us -> 31 us  [swapped(): return lax.ppermute(block, axis, [(i, size - 1 - i) for i in range(size)])]
    all_to_all x1, waiting for transfers between devices: 7.61 us -> 24.4 us  [body(): lax.all_to_all(block, ('yh', 'x', 'chip'), split_axis=0, concat_axis=0, t...]
    pallas_call x3 -> x4, Pallas kernels: 5.97 us -> 7.61 us  [the longest x1 3.71 us: filter_bank(): pl.pallas_call(filter_kernel, in_specs=[pl.BlockSpec(memory_space=pltpu.H...]
    unnamed x10, local copies, waits for them, and re-layouts: 4.11 us -> 2.8 us
  transfers between devices with their start and end apart: 12 -> 12, of which waited for: 9 -> 6; matrix products, arithmetic and copies ran while one was open for 4% -> 4% of each run, Pallas kernels for 10% -> 13%
where the time goes in v4:
time: 119 us
  waiting for transfers between devices  55.7 us (47%)
  starting transfers between devices  29.6 us (25%)
  Pallas kernels  24.9 us (21%)
  local copies, waits for them, and re-layouts  5.48 us (5%)
  other arithmetic  3.01 us (3%)
    ppermute x9, waiting for transfers between devices, swapped(): return lax.ppermute(block, axis, [(i, size - 1 - i) for i in range(size)])  31 us
    all_to_all x1, waiting for transfers between devices, body(): lax.all_to_all(block, ('yh', 'x', 'chip'), split_axis=0, concat_axis=0, t...  24.4 us
    all_to_all x1, starting transfers between devices, body(): lax.all_to_all(block, ('yh', 'x', 'chip'), split_axis=0, concat_axis=0, t...  13.9 us
    pallas_call x3, Pallas kernels, correlate(): pl.pallas_call(functools.partial(correlate_kernel, scale, forms), grid=(l...  12.6 us
    ppermute x9, starting transfers between devices, swapped(): return lax.ppermute(block, axis, [(i, size - 1 - i) for i in range(size)])  6.64 us
    all_to_all x1, starting transfers between devices, body(): lax.all_to_all(block, ('x', 'chip'), split_axis=0, concat_axis=0, tiled=T...  5.62 us
    pallas_call x4, Pallas kernels, spectra(): pl.pallas_call(functools.partial(spectra_kernel, width), out_shape=[jax.S...  4.67 us
    pallas_call x1, Pallas kernels, filter_bank(): pl.pallas_call(filter_kernel, in_specs=[pl.BlockSpec(memory_space=pltpu.H...  3.71 us
  transfers between devices with their start and end apart: 12, of which 6 were waited for; matrix products, arithmetic and copies ran while one was open for 4% of the time, Pallas kernels for 13%

profile of v4, /device:TPU:38, one launch (start us, length us, event | category | flops | bytes accessed | tf_op | source)
XLA Modules:
  0.0 119.0 jit_solution(9469900115221811062)
XLA Ops:
  0.0 1.0 slice.9
  1.0 3.5 %collective-permute-start = (bf16[8,4,2048]{2,1,0:T(4,128)(2,1)S(1)}, bf16[8,4,2048]{2,1,0:T(4,128)(2,1)S(1)}, u32[]{:S(2)}, u32[]{:S(2)}) collective-permute-start(bf16[8,4,2048]{2,1,0:T(4,128)(2,1)S(1)} %slice.9), channel_id=1, source_target_pairs={{0,1},{2,3},{4,5},{6,7},{8,9},{10,11},{12,13},{14,15},{16,17},{18,... | collective-permute-start | bytes 393224 | tf_op jit(solution)/shard_map/ppermute | solution.py:22
  4.8 1.1 fusion.6
  6.6 0.3 subtract_convert_fusion
  7.0 0.3 collective-permute-done.hist_ref
  7.3 1.0 copy-done.2
  8.3 3.7 %filter_bank.1 = (bf16[1024,512]{1,0:T(8,128)(2,1)S(1)}, bf16[1024,512]{1,0:T(8,128)(2,1)S(1)}, bf16[1024,1024]{1,0:T(8,128)(2,1)S(1)}) custom-call(bf16[8,128,2048]{2,1,0:T(8,128)(2,1)S(1)} %copy-done.2, bf16[8,4,2048]{2,1,0:T(4,128)(2,1)S(1)} %collective-permute-done.hist_ref, f32[4,2048]{1,0:T(4,128)S(1)} %copy-done.3), custom_call_target="tpu_custom_call" | custom-call | flops 41943040 | bytes 8388608 | tf_op jit(solution)/shard_map/filter_bank/pallas_call | solution.py:94
  12.0 1.1 spectra.7
  13.2 1.1 spectra.6
  14.3 0.6 collective-permute-start.6
  14.9 1.2 %spectra.5 = (bf16[64,16,128]{2,1,0:T(8,128)(2,1)S(1)}, bf16[64,16,128]{2,1,0:T(8,128)(2,1)S(1)}) custom-call(bf16[256,1024]{1,0:T(8,128)(2,1)S(1)} %pad_maximum_fusion.2.table_ref, bf16[1024,1024]{1,0:T(8,128)(2,1)S(1)} %get-tuple-element.22.filt_ref), custom_call_target="tpu_custom_call" | custom-call | flops 536870912 | bytes 2097152 | tf_op jit(solution)/shard_map/spectra/pallas_call | solution.py:133
  16.3 1.7 %merge.2.refs_2_ = bf16[64,6,16,128]{3,2,1,0:T(8,128)(2,1)} custom-call(s32[3]{0:T(128)S(1)} %pad_add_fusion.place_ref, bf16[64,16,128]{2,1,0:T(8,128)(2,1)S(1)} %get-tuple-element.30.refs_0_, bf16[64,16,128]{2,1,0:T(8,128)(2,1)S(1)} %get-tuple-element.32.refs_1_, bf16[64,16,128]{2,1,0:T(8,128)(2,1)S(1)} %collective-permute-done.6.refs_2_, ...), custom_call_target="tpu_custom_call" | custom-call | bytes 2097152 | tf_op jit(solution)/shard_map/merge/pallas_call | solution.py:188
  18.0 1.6 %merge.3 = bf16[64,6,16,128]{3,2,1,0:T(8,128)(2,1)} custom-call(s32[3]{0:T(128)S(1)} %pad_add_fusion.place_ref, bf16[64,16,128]{2,1,0:T(8,128)(2,1)S(1)} %get-tuple-element.27.refs_0_, bf16[64,16,128]{2,1,0:T(8,128)(2,1)S(1)} %collective-permute-done.5.refs_1_, bf16[64,6,16,128]{3,2,1,0:T(8,128)(2,1)} %merge.2.refs_2_), custom_call_target="tpu_custom_call", output_to_operand_aliasing={{}: (3, {})} | custom-call | bytes 1048576 | tf_op jit(solution)/shard_map/merge/pallas_call | solution.py:188
  19.6 13.9 %all-to-all-start.1 = ((bf16[64,6,16,128]{3,2,1,0:T(8,128)(2,1)}), bf16[64,6,16,128]{3,2,1,0:T(8,128)(2,1)S(1)}, u32[]{:S(2)}, u32[]{:S(2)}) async-start(bf16[64,6,16,128]{3,2,1,0:T(8,128)(2,1)} %merge.3), calls=%async_computation.1 | async-start | bytes 3145728 | tf_op jit(solution)/shard_map/all_to_all | solution.py:328
  33.5 1.6 %copy-done.1 = bf16[1024,1024]{1,0:T(8,128)(2,1)S(1)} copy-done((bf16[1024,1024]{1,0:T(8,128)(2,1)S(1)}, bf16[1024,1024]{1,0:T(8,128)(2,1)}, u32[]{:S(2)}) %copy-start.1) | copy-done | bytes 2097176
  35.1 1.2 %spectra.4 = (bf16[64,16,128]{2,1,0:T(8,128)(2,1)S(1)}, bf16[64,16,128]{2,1,0:T(8,128)(2,1)S(1)}) custom-call(bf16[256,1024]{1,0:T(8,128)(2,1)S(1)} %pad_maximum_fusion.1.table_ref, bf16[1024,1024]{1,0:T(8,128)(2,1)S(1)} %copy-done.1), custom_call_target="tpu_custom_call" | custom-call | flops 536870912 | bytes 2097152 | tf_op jit(solution)/shard_map/spectra/pallas_call | solution.py:133
  36.5 1.5 %collective-permute-done.1.refs_1_ = bf16[64,16,128]{2,1,0:T(8,128)(2,1)S(1)} collective-permute-done((bf16[64,16,128]{2,1,0:T(8,128)(2,1)S(1)}, bf16[64,16,128]{2,1,0:T(8,128)(2,1)S(1)}, u32[]{:S(2)}, u32[]{:S(2)}) %collective-permute-start.1) | collective-permute-done | bytes 262176 | tf_op jit(solution)/shard_map/ppermute | solution.py:27
  38.0 0.6 split.1
  38.6 3.3 %collective-permute-start.3 = (bf16[32,2,16,128]{3,2,1,0:T(8,128)(2,1)S(1)}, bf16[32,2,16,128]{3,2,1,0:T(8,128)(2,1)S(1)}, u32[]{:S(2)}, u32[]{:S(2)}) collective-permute-start(bf16[32,2,16,128]{3,2,1,0:T(8,128)(2,1)S(1)} %get-tuple-element.26), channel_id=1, source_target_pairs={{0,129},{1,128},{128,1},{129,0},{2,131},{3,130},{130,3},{131,2},{4... | collective-permute-start | bytes 786440 | tf_op jit(solution)/shard_map/ppermute | solution.py:27
  41.9 9.0 %collective-permute-done.3 = bf16[32,2,16,128]{3,2,1,0:T(8,128)(2,1)S(1)} collective-permute-done((bf16[32,2,16,128]{3,2,1,0:T(8,128)(2,1)S(1)}, bf16[32,2,16,128]{3,2,1,0:T(8,128)(2,1)S(1)}, u32[]{:S(2)}, u32[]{:S(2)}) %collective-permute-start.3) | collective-permute-done | bytes 262176 | tf_op jit(solution)/shard_map/ppermute | solution.py:27
  50.9 0.4 collective-permute-start.4
  51.3 24.4 %all-to-all-done.1.refs_0_.refs_2_.refs_4_.refs_6_ = bf16[64,6,16,128]{3,2,1,0:T(8,128)(2,1)S(1)} async-done(((bf16[64,6,16,128]{3,2,1,0:T(8,128)(2,1)}), bf16[64,6,16,128]{3,2,1,0:T(8,128)(2,1)S(1)}, u32[]{:S(2)}, u32[]{:S(2)}) %all-to-all-start.1) | async-done | bytes 1572896 | tf_op jit(solution)/shard_map/all_to_all | solution.py:328
  75.7 1.3 %slice.13 = bf16[64,4,16,128]{3,2,1,0:T(8,128)(2,1)} slice(bf16[64,6,16,128]{3,2,1,0:T(8,128)(2,1)S(1)} %all-to-all-done.1.refs_0_.refs_2_.refs_4_.refs_6_), slice={[0:64], [0:4], [0:16], [0:128]} | slice | bytes 2097152 | tf_op jit(solution)/shard_map/slice | solution.py:330
  77.0 0.9 collective-permute-start.9
  77.9 1.1 pad_maximum_fusion
  79.0 5.6 %all-to-all-start = ((bf16[32,4,2,16,128]{4,3,2,1,0:T(8,128)(2,1)}), bf16[32,4,2,16,128]{4,3,2,1,0:T(8,128)(2,1)S(1)}, u32[]{:S(2)}, u32[]{:S(2)}) async-start(bf16[32,4,2,16,128]{4,3,2,1,0:T(8,128)(2,1)} %pad_maximum_fusion), calls=%async_computation | async-start | bytes 2097152 | tf_op jit(solution)/shard_map/all_to_all | solution.py:337
  84.7 1.2 %collective-permute-start.8 = (bf16[64,2,16,128]{3,2,1,0:T(8,128)(2,1)S(1)}, bf16[64,2,16,128]{3,2,1,0:T(8,128)(2,1)S(1)}, u32[]{:S(2)}, u32[]{:S(2)}) collective-permute-start(bf16[64,2,16,128]{3,2,1,0:T(8,128)(2,1)S(1)} %slice.12), channel_id=1, source_target_pairs={{0,1},{1,0},{2,3},{3,2},{4,5},{5,4},{6,7},{7,6},{8,9},{9,8},{10,11... | collective-permute-start | bytes 1572872 | tf_op jit(solution)/shard_map/ppermute | solution.py:27
  85.9 17.5 %collective-permute-done.9.refs_1_.refs_3_.refs_5_.refs_7_ = bf16[64,4,16,128]{3,2,1,0:T(8,128)(2,1)} collective-permute-done((bf16[64,4,16,128]{3,2,1,0:T(8,128)(2,1)}, bf16[64,4,16,128]{3,2,1,0:T(8,128)(2,1)}, u32[]{:S(2)}, u32[]{:S(2)}) %collective-permute-start.9) | collective-permute-done | bytes 1048608 | tf_op jit(solution)/shard_map/ppermute | solution.py:27
  103.4 6.0 %correlate.3.refs_4_ = bf16[2,4,512,1024]{3,2,1,0:T(8,128)(2,1)} custom-call(s32[3]{0:T(128)S(1)} %pad_add_fusion.place_ref, bf16[64,6,16,128]{3,2,1,0:T(8,128)(2,1)S(1)} %all-to-all-done.1.refs_0_.refs_2_.refs_4_.refs_6_, bf16[64,4,16,128]{3,2,1,0:T(8,128)(2,1)} %collective-permute-done.9.refs_1_.refs_3_.refs_5_.refs_7_, ...), custom_call_target="tpu_custom_call" | custom-call | flops 8589934592 | bytes 4194304 | tf_op jit(solution)/shard_map/correlate/pallas_call | solution.py:285
  109.4 3.0 %collective-permute-done.8.refs_1_.refs_3_ = bf16[64,2,16,128]{3,2,1,0:T(8,128)(2,1)S(1)} collective-permute-done((bf16[64,2,16,128]{3,2,1,0:T(8,128)(2,1)S(1)}, bf16[64,2,16,128]{3,2,1,0:T(8,128)(2,1)S(1)}, u32[]{:S(2)}, u32[]{:S(2)}) %collective-permute-start.8) | collective-permute-done | bytes 524320 | tf_op jit(solution)/shard_map/ppermute | solution.py:27
  112.4 3.3 %correlate.4.refs_2_ = bf16[2,4,512,1024]{3,2,1,0:T(8,128)(2,1)} custom-call(s32[3]{0:T(128)S(1)} %pad_add_fusion.place_ref, bf16[64,6,16,128]{3,2,1,0:T(8,128)(2,1)S(1)} %all-to-all-done.1.refs_0_.refs_2_.refs_4_.refs_6_, bf16[64,2,16,128]{3,2,1,0:T(8,128)(2,1)S(1)} %collective-permute-done.8.refs_1_.refs_3_, ...), custom_call_target="tpu_custom_call", output_to_operand_aliasing={{}: (5, {})} | custom-call | flops 4294967296 | bytes 2097152 | tf_op jit(solution)/shard_map/correlate/pallas_call | solution.py:285
  115.7 3.3 %correlate.5 = bf16[2,4,512,1024]{3,2,1,0:T(8,128)(2,1)} custom-call(s32[3]{0:T(128)S(1)} %pad_add_fusion.place_ref, bf16[32,4,2,16,128]{4,3,2,1,0:T(8,128)(2,1)S(1)} %all-to-all-done.refs_0_.refs_1_, bf16[32,4,2,16,128]{4,3,2,1,0:T(8,128)(2,1)S(1)} %all-to-all-done.refs_0_.refs_1_, ...), custom_call_target="tpu_custom_call", output_to_operand_aliasing={{}: (3, {})} | custom-call | flops 4294967296 | bytes 2097152 | tf_op jit(solution)/shard_map/correlate/pallas_call | solution.py:285
  (32 shorter events, 1.4 us)
Async XLA Ops:
  1.0 6.2 %collective-permute-start = (bf16[8,4,2048]{2,1,0:T(4,128)(2,1)S(1)}, bf16[8,4,2048]{2,1,0:T(4,128)(2,1)S(1)}, u32[]{:S(2)}, u32[]{:S(2)}) collective-permute-start(bf16[8,4,2048]{2,1,0:T(4,128)(2,1)S(1)} %slice.9), channel_id=1, source_target_pairs={{0,1},{2,3},{4,5},{6,7},{8,9},{10,11},{12,13},{14,15},{16,17},{18,... | collective-permute-start | bytes 393224 | tf_op jit(solution)/shard_map/ppermute | solution.py:22
  6.1 2.2 %copy-start.2 = (bf16[8,128,2048]{2,1,0:T(8,128)(2,1)S(1)}, bf16[8,128,2048]{2,1,0:T(8,128)(2,1)}, u32[]{:S(2)}) copy-start(bf16[8,128,2048]{2,1,0:T(8,128)(2,1)} %source_ref.1) | copy-start | bytes 12582916
  6.1 2.2 %copy-start.3 = (f32[4,2048]{1,0:T(4,128)S(1)}, f32[4,2048]{1,0:T(4,128)}, u32[]{:S(2)}) copy-start(f32[4,2048]{1,0:T(4,128)} %taps_ref.1) | copy-start | bytes 98308
  12.0 2.9 %copy-start = (bf16[1024,1024]{1,0:T(8,128)(2,1)}, bf16[1024,1024]{1,0:T(8,128)(2,1)S(1)}, u32[]{:S(2)}) copy-start(bf16[1024,1024]{1,0:T(8,128)(2,1)S(1)} %get-tuple-element.22.filt_ref) | copy-start | bytes 6291460
  13.1 3.2 %collective-permute-start.7 = (bf16[64,16,128]{2,1,0:T(8,128)(2,1)S(1)}, bf16[64,16,128]{2,1,0:T(8,128)(2,1)S(1)}, u32[]{:S(2)}, u32[]{:S(2)}) collective-permute-start(bf16[64,16,128]{2,1,0:T(8,128)(2,1)S(1)} %get-tuple-element.34), channel_id=1, source_target_pairs={{0,2},{2,0},{1,3},{3,1},{4,6},{6,4},{5,7},{7,5},{8,10},{10,8},{9,1... | collective-permute-start | bytes 786440 | tf_op jit(solution)/shard_map/ppermute | solution.py:27
  14.3 2.0 %collective-permute-start.6 = (bf16[64,16,128]{2,1,0:T(8,128)(2,1)S(1)}, bf16[64,16,128]{2,1,0:T(8,128)(2,1)S(1)}, u32[]{:S(2)}, u32[]{:S(2)}) collective-permute-start(bf16[64,16,128]{2,1,0:T(8,128)(2,1)S(1)} %get-tuple-element.33), channel_id=1, source_target_pairs={{0,2},{2,0},{1,3},{3,1},{4,6},{6,4},{5,7},{7,5},{8,10},{10,8},{9,1... | collective-permute-start | bytes 786440 | tf_op jit(solution)/shard_map/ppermute | solution.py:27
  16.1 1.9 %collective-permute-start.5 = (bf16[64,16,128]{2,1,0:T(8,128)(2,1)S(1)}, bf16[64,16,128]{2,1,0:T(8,128)(2,1)S(1)}, u32[]{:S(2)}, u32[]{:S(2)}) collective-permute-start(bf16[64,16,128]{2,1,0:T(8,128)(2,1)S(1)} %get-tuple-element.28), channel_id=1, source_target_pairs={{0,2},{2,0},{1,3},{3,1},{4,6},{6,4},{5,7},{7,5},{8,10},{10,8},{9,1... | collective-permute-start | bytes 786440 | tf_op jit(solution)/shard_map/ppermute | solution.py:27
  19.6 56.1 %all-to-all-start.1 = ((bf16[64,6,16,128]{3,2,1,0:T(8,128)(2,1)}), bf16[64,6,16,128]{3,2,1,0:T(8,128)(2,1)S(1)}, u32[]{:S(2)}, u32[]{:S(2)}) async-start(bf16[64,6,16,128]{3,2,1,0:T(8,128)(2,1)} %merge.3), calls=%async_computation.1 | async-start | bytes 3145728 | tf_op jit(solution)/shard_map/all_to_all | solution.py:328
  33.5 1.6 %copy-start.1 = (bf16[1024,1024]{1,0:T(8,128)(2,1)S(1)}, bf16[1024,1024]{1,0:T(8,128)(2,1)}, u32[]{:S(2)}) copy-start(bf16[1024,1024]{1,0:T(8,128)(2,1)} %copy-done) | copy-start | bytes 6291460
  36.4 1.6 %collective-permute-start.1 = (bf16[64,16,128]{2,1,0:T(8,128)(2,1)S(1)}, bf16[64,16,128]{2,1,0:T(8,128)(2,1)S(1)}, u32[]{:S(2)}, u32[]{:S(2)}) collective-permute-start(bf16[64,16,128]{2,1,0:T(8,128)(2,1)S(1)} %get-tuple-element.24), channel_id=1, source_target_pairs={{0,2},{2,0},{1,3},{3,1},{4,6},{6,4},{5,7},{7,5},{8,10},{10,8},{9,1... | collective-permute-start | bytes 786440 | tf_op jit(solution)/shard_map/ppermute | solution.py:27
  38.6 12.3 %collective-permute-start.3 = (bf16[32,2,16,128]{3,2,1,0:T(8,128)(2,1)S(1)}, bf16[32,2,16,128]{3,2,1,0:T(8,128)(2,1)S(1)}, u32[]{:S(2)}, u32[]{:S(2)}) collective-permute-start(bf16[32,2,16,128]{3,2,1,0:T(8,128)(2,1)S(1)} %get-tuple-element.26), channel_id=1, source_target_pairs={{0,129},{1,128},{128,1},{129,0},{2,131},{3,130},{130,3},{131,2},{4... | collective-permute-start | bytes 786440 | tf_op jit(solution)/shard_map/ppermute | solution.py:27
  41.9 35.9 %collective-permute-start.2 = (bf16[32,2,16,128]{3,2,1,0:T(8,128)(2,1)S(1)}, bf16[32,2,16,128]{3,2,1,0:T(8,128)(2,1)S(1)}, u32[]{:S(2)}, u32[]{:S(2)}) collective-permute-start(bf16[32,2,16,128]{3,2,1,0:T(8,128)(2,1)S(1)} %get-tuple-element.25), channel_id=1, source_target_pairs={{0,1},{1,0},{2,3},{3,2},{4,5},{5,4},{6,7},{7,6},{8,9},{9,8},{10,11... | collective-permute-start | bytes 786440 | tf_op jit(solution)/shard_map/ppermute | solution.py:27
  50.9 26.9 %collective-permute-start.4 = (bf16[32,2,16,128]{3,2,1,0:T(8,128)(2,1)S(1)}, bf16[32,2,16,128]{3,2,1,0:T(8,128)(2,1)S(1)}, u32[]{:S(2)}, u32[]{:S(2)}) collective-permute-start(bf16[32,2,16,128]{3,2,1,0:T(8,128)(2,1)S(1)} %collective-permute-done.3), channel_id=1, source_target_pairs={{0,1},{1,0},{2,3},{3,2},{4,5},{5,4},{6,7},{7,6},{8,9},{9,8},{10,11... | collective-permute-start | bytes 786440 | tf_op jit(solution)/shard_map/ppermute | solution.py:27
  77.0 26.4 %collective-permute-start.9 = (bf16[64,4,16,128]{3,2,1,0:T(8,128)(2,1)}, bf16[64,4,16,128]{3,2,1,0:T(8,128)(2,1)}, u32[]{:S(2)}, u32[]{:S(2)}) collective-permute-start(bf16[64,4,16,128]{3,2,1,0:T(8,128)(2,1)} %slice.13), channel_id=1, source_target_pairs={{0,1},{1,0},{2,3},{3,2},{4,5},{5,4},{6,7},{7,6},{8,9},{9,8},{10,11... | collective-permute-start | bytes 3145736 | tf_op jit(solution)/shard_map/ppermute | solution.py:27
  79.0 36.7 %all-to-all-start = ((bf16[32,4,2,16,128]{4,3,2,1,0:T(8,128)(2,1)}), bf16[32,4,2,16,128]{4,3,2,1,0:T(8,128)(2,1)S(1)}, u32[]{:S(2)}, u32[]{:S(2)}) async-start(bf16[32,4,2,16,128]{4,3,2,1,0:T(8,128)(2,1)} %pad_maximum_fusion), calls=%async_computation | async-start | bytes 2097152 | tf_op jit(solution)/shard_map/all_to_all | solution.py:337
  84.7 27.7 %collective-permute-start.8 = (bf16[64,2,16,128]{3,2,1,0:T(8,128)(2,1)S(1)}, bf16[64,2,16,128]{3,2,1,0:T(8,128)(2,1)S(1)}, u32[]{:S(2)}, u32[]{:S(2)}) collective-permute-start(bf16[64,2,16,128]{3,2,1,0:T(8,128)(2,1)S(1)} %slice.12), channel_id=1, source_target_pairs={{0,1},{1,0},{2,3},{3,2},{4,5},{5,4},{6,7},{7,6},{8,9},{9,8},{10,11... | collective-permute-start | bytes 1572872 | tf_op jit(solution)/shard_map/ppermute | solution.py:27

commit v5 on v4

--- a/solution.py
+++ b/solution.py
@@ -11,7 +11,7 @@
 CH = 512
 LANES = 128
 ROWS = 32
-COLUMNS = 512
+COLUMNS = 1024
 WEIGHT = 4
 MIB = 1024 * 1024
 

time: 119 us -> 119 us (level)
  no operation moved by 1% of the time
where the time goes in v5:
time: 119 us
  waiting for transfers between devices  56 us (47%)
  starting transfers between devices  29.6 us (25%)
  Pallas kernels  24.6 us (21%)
  local copies, waits for them, and re-layouts  5.48 us (5%)
  other arithmetic  3.01 us (3%)
    ppermute x9, waiting for transfers between devices, swapped(): return lax.ppermute(block, axis, [(i, size - 1 - i) for i in range(size)])  31.3 us
    all_to_all x1, waiting for transfers between devices, body(): lax.all_to_all(block, ('yh', 'x', 'chip'), split_axis=0, concat_axis=0, t...  24.4 us
    all_to_all x1, starting transfers between devices, body(): lax.all_to_all(block, ('yh', 'x', 'chip'), split_axis=0, concat_axis=0, t...  13.9 us
    pallas_call x3, Pallas kernels, correlate(): pl.pallas_call(functools.partial(correlate_kernel, scale, forms), grid=(l...  12.3 us
    ppermute x9, starting transfers between devices, swapped(): return lax.ppermute(block, axis, [(i, size - 1 - i) for i in range(size)])  6.64 us
    all_to_all x1, starting transfers between devices, body(): lax.all_to_all(block, ('x', 'chip'), split_axis=0, concat_axis=0, tiled=T...  5.62 us
    pallas_call x4, Pallas kernels, spectra(): pl.pallas_call(functools.partial(spectra_kernel, width), out_shape=[jax.S...  4.67 us
    pallas_call x1, Pallas kernels, filter_bank(): pl.pallas_call(filter_kernel, in_specs=[pl.BlockSpec(memory_space=pltpu.H...  3.71 us
  transfers between devices with their start and end apart: 12, of which 6 were waited for; matrix products, arithmetic and copies ran while one was open for 4% of the time, Pallas kernels for 13%

profile of v5, /device:TPU:38, one launch (start us, length us, event | category | flops | bytes accessed | tf_op | source)
XLA Modules:
  0.0 119.0 jit_solution(14601165689875063870)
XLA Ops:
  0.0 1.0 slice.9
  1.0 3.5 %collective-permute-start = (bf16[8,4,2048]{2,1,0:T(4,128)(2,1)S(1)}, bf16[8,4,2048]{2,1,0:T(4,128)(2,1)S(1)}, u32[]{:S(2)}, u32[]{:S(2)}) collective-permute-start(bf16[8,4,2048]{2,1,0:T(4,128)(2,1)S(1)} %slice.9), channel_id=1, source_target_pairs={{0,1},{2,3},{4,5},{6,7},{8,9},{10,11},{12,13},{14,15},{16,17},{18,... | collective-permute-start | bytes 393224 | tf_op jit(solution)/shard_map/ppermute | solution.py:22
  4.8 1.1 fusion.6
  6.6 0.3 subtract_convert_fusion
  7.0 0.3 collective-permute-done.hist_ref
  7.3 1.0 copy-done.2
  8.3 3.7 %filter_bank.1 = (bf16[1024,512]{1,0:T(8,128)(2,1)S(1)}, bf16[1024,512]{1,0:T(8,128)(2,1)S(1)}, bf16[1024,1024]{1,0:T(8,128)(2,1)S(1)}) custom-call(bf16[8,128,2048]{2,1,0:T(8,128)(2,1)S(1)} %copy-done.2, bf16[8,4,2048]{2,1,0:T(4,128)(2,1)S(1)} %collective-permute-done.hist_ref, f32[4,2048]{1,0:T(4,128)S(1)} %copy-done.3), custom_call_target="tpu_custom_call" | custom-call | flops 41943040 | bytes 8388608 | tf_op jit(solution)/shard_map/filter_bank/pallas_call | solution.py:94
  12.0 1.1 spectra.7
  13.2 1.1 spectra.6
  14.3 0.6 collective-permute-start.6
  14.9 1.2 %spectra.5 = (bf16[64,16,128]{2,1,0:T(8,128)(2,1)S(1)}, bf16[64,16,128]{2,1,0:T(8,128)(2,1)S(1)}) custom-call(bf16[256,1024]{1,0:T(8,128)(2,1)S(1)} %pad_maximum_fusion.2.table_ref, bf16[1024,1024]{1,0:T(8,128)(2,1)S(1)} %get-tuple-element.22.filt_ref), custom_call_target="tpu_custom_call" | custom-call | flops 536870912 | bytes 2097152 | tf_op jit(solution)/shard_map/spectra/pallas_call | solution.py:133
  16.3 1.7 %merge.2.refs_2_ = bf16[64,6,16,128]{3,2,1,0:T(8,128)(2,1)} custom-call(s32[3]{0:T(128)S(1)} %pad_add_fusion.place_ref, bf16[64,16,128]{2,1,0:T(8,128)(2,1)S(1)} %get-tuple-element.30.refs_0_, bf16[64,16,128]{2,1,0:T(8,128)(2,1)S(1)} %get-tuple-element.32.refs_1_, bf16[64,16,128]{2,1,0:T(8,128)(2,1)S(1)} %collective-permute-done.6.refs_2_, ...), custom_call_target="tpu_custom_call" | custom-call | bytes 2097152 | tf_op jit(solution)/shard_map/merge/pallas_call | solution.py:188
  18.0 1.6 %merge.3 = bf16[64,6,16,128]{3,2,1,0:T(8,128)(2,1)} custom-call(s32[3]{0:T(128)S(1)} %pad_add_fusion.place_ref, bf16[64,16,128]{2,1,0:T(8,128)(2,1)S(1)} %get-tuple-element.27.refs_0_, bf16[64,16,128]{2,1,0:T(8,128)(2,1)S(1)} %collective-permute-done.5.refs_1_, bf16[64,6,16,128]{3,2,1,0:T(8,128)(2,1)} %merge.2.refs_2_), custom_call_target="tpu_custom_call", output_to_operand_aliasing={{}: (3, {})} | custom-call | bytes 1048576 | tf_op jit(solution)/shard_map/merge/pallas_call | solution.py:188
  19.6 13.9 %all-to-all-start.1 = ((bf16[64,6,16,128]{3,2,1,0:T(8,128)(2,1)}), bf16[64,6,16,128]{3,2,1,0:T(8,128)(2,1)S(1)}, u32[]{:S(2)}, u32[]{:S(2)}) async-start(bf16[64,6,16,128]{3,2,1,0:T(8,128)(2,1)} %merge.3), calls=%async_computation.1 | async-start | bytes 3145728 | tf_op jit(solution)/shard_map/all_to_all | solution.py:328
  33.5 1.6 %copy-done.1 = bf16[1024,1024]{1,0:T(8,128)(2,1)S(1)} copy-done((bf16[1024,1024]{1,0:T(8,128)(2,1)S(1)}, bf16[1024,1024]{1,0:T(8,128)(2,1)}, u32[]{:S(2)}) %copy-start.1) | copy-done | bytes 2097176
  35.1 1.2 %spectra.4 = (bf16[64,16,128]{2,1,0:T(8,128)(2,1)S(1)}, bf16[64,16,128]{2,1,0:T(8,128)(2,1)S(1)}) custom-call(bf16[256,1024]{1,0:T(8,128)(2,1)S(1)} %pad_maximum_fusion.1.table_ref, bf16[1024,1024]{1,0:T(8,128)(2,1)S(1)} %copy-done.1), custom_call_target="tpu_custom_call" | custom-call | flops 536870912 | bytes 2097152 | tf_op jit(solution)/shard_map/spectra/pallas_call | solution.py:133
  36.5 1.5 %collective-permute-done.1.refs_1_ = bf16[64,16,128]{2,1,0:T(8,128)(2,1)S(1)} collective-permute-done((bf16[64,16,128]{2,1,0:T(8,128)(2,1)S(1)}, bf16[64,16,128]{2,1,0:T(8,128)(2,1)S(1)}, u32[]{:S(2)}, u32[]{:S(2)}) %collective-permute-start.1) | collective-permute-done | bytes 262176 | tf_op jit(solution)/shard_map/ppermute | solution.py:27
  38.0 0.6 split.1
  38.6 3.3 %collective-permute-start.3 = (bf16[32,2,16,128]{3,2,1,0:T(8,128)(2,1)S(1)}, bf16[32,2,16,128]{3,2,1,0:T(8,128)(2,1)S(1)}, u32[]{:S(2)}, u32[]{:S(2)}) collective-permute-start(bf16[32,2,16,128]{3,2,1,0:T(8,128)(2,1)S(1)} %get-tuple-element.26), channel_id=1, source_target_pairs={{0,129},{1,128},{128,1},{129,0},{2,131},{3,130},{130,3},{131,2},{4... | collective-permute-start | bytes 786440 | tf_op jit(solution)/shard_map/ppermute | solution.py:27
  41.9 9.0 %collective-permute-done.3 = bf16[32,2,16,128]{3,2,1,0:T(8,128)(2,1)S(1)} collective-permute-done((bf16[32,2,16,128]{3,2,1,0:T(8,128)(2,1)S(1)}, bf16[32,2,16,128]{3,2,1,0:T(8,128)(2,1)S(1)}, u32[]{:S(2)}, u32[]{:S(2)}) %collective-permute-start.3) | collective-permute-done | bytes 262176 | tf_op jit(solution)/shard_map/ppermute | solution.py:27
  50.9 0.4 collective-permute-start.4
  51.3 24.4 %all-to-all-done.1.refs_0_.refs_2_.refs_4_.refs_6_ = bf16[64,6,16,128]{3,2,1,0:T(8,128)(2,1)S(1)} async-done(((bf16[64,6,16,128]{3,2,1,0:T(8,128)(2,1)}), bf16[64,6,16,128]{3,2,1,0:T(8,128)(2,1)S(1)}, u32[]{:S(2)}, u32[]{:S(2)}) %all-to-all-start.1) | async-done | bytes 1572896 | tf_op jit(solution)/shard_map/all_to_all | solution.py:328
  75.7 1.3 %slice.13 = bf16[64,4,16,128]{3,2,1,0:T(8,128)(2,1)} slice(bf16[64,6,16,128]{3,2,1,0:T(8,128)(2,1)S(1)} %all-to-all-done.1.refs_0_.refs_2_.refs_4_.refs_6_), slice={[0:64], [0:4], [0:16], [0:128]} | slice | bytes 2097152 | tf_op jit(solution)/shard_map/slice | solution.py:330
  77.0 0.9 collective-permute-start.9
  77.9 1.1 pad_maximum_fusion
  79.0 5.6 %all-to-all-start = ((bf16[32,4,2,16,128]{4,3,2,1,0:T(8,128)(2,1)}), bf16[32,4,2,16,128]{4,3,2,1,0:T(8,128)(2,1)S(1)}, u32[]{:S(2)}, u32[]{:S(2)}) async-start(bf16[32,4,2,16,128]{4,3,2,1,0:T(8,128)(2,1)} %pad_maximum_fusion), calls=%async_computation | async-start | bytes 2097152 | tf_op jit(solution)/shard_map/all_to_all | solution.py:337
  84.7 1.2 %collective-permute-start.8 = (bf16[64,2,16,128]{3,2,1,0:T(8,128)(2,1)S(1)}, bf16[64,2,16,128]{3,2,1,0:T(8,128)(2,1)S(1)}, u32[]{:S(2)}, u32[]{:S(2)}) collective-permute-start(bf16[64,2,16,128]{3,2,1,0:T(8,128)(2,1)S(1)} %slice.12), channel_id=1, source_target_pairs={{0,1},{1,0},{2,3},{3,2},{4,5},{5,4},{6,7},{7,6},{8,9},{9,8},{10,11... | collective-permute-start | bytes 1572872 | tf_op jit(solution)/shard_map/ppermute | solution.py:27
  85.9 17.5 %collective-permute-done.9.refs_1_.refs_3_.refs_5_.refs_7_ = bf16[64,4,16,128]{3,2,1,0:T(8,128)(2,1)} collective-permute-done((bf16[64,4,16,128]{3,2,1,0:T(8,128)(2,1)}, bf16[64,4,16,128]{3,2,1,0:T(8,128)(2,1)}, u32[]{:S(2)}, u32[]{:S(2)}) %collective-permute-start.9) | collective-permute-done | bytes 1048608 | tf_op jit(solution)/shard_map/ppermute | solution.py:27
  103.4 5.7 %correlate.3.refs_4_ = bf16[2,4,512,1024]{3,2,1,0:T(8,128)(2,1)} custom-call(s32[3]{0:T(128)S(1)} %pad_add_fusion.place_ref, bf16[64,6,16,128]{3,2,1,0:T(8,128)(2,1)S(1)} %all-to-all-done.1.refs_0_.refs_2_.refs_4_.refs_6_, bf16[64,4,16,128]{3,2,1,0:T(8,128)(2,1)} %collective-permute-done.9.refs_1_.refs_3_.refs_5_.refs_7_, ...), custom_call_target="tpu_custom_call" | custom-call | flops 8589934592 | bytes 4194304 | tf_op jit(solution)/shard_map/correlate/pallas_call | solution.py:285
  109.1 3.3 %collective-permute-done.8.refs_1_.refs_3_ = bf16[64,2,16,128]{3,2,1,0:T(8,128)(2,1)S(1)} collective-permute-done((bf16[64,2,16,128]{3,2,1,0:T(8,128)(2,1)S(1)}, bf16[64,2,16,128]{3,2,1,0:T(8,128)(2,1)S(1)}, u32[]{:S(2)}, u32[]{:S(2)}) %collective-permute-start.8) | collective-permute-done | bytes 524320 | tf_op jit(solution)/shard_map/ppermute | solution.py:27
  112.4 3.3 %correlate.4.refs_2_ = bf16[2,4,512,1024]{3,2,1,0:T(8,128)(2,1)} custom-call(s32[3]{0:T(128)S(1)} %pad_add_fusion.place_ref, bf16[64,6,16,128]{3,2,1,0:T(8,128)(2,1)S(1)} %all-to-all-done.1.refs_0_.refs_2_.refs_4_.refs_6_, bf16[64,2,16,128]{3,2,1,0:T(8,128)(2,1)S(1)} %collective-permute-done.8.refs_1_.refs_3_, ...), custom_call_target="tpu_custom_call", output_to_operand_aliasing={{}: (5, {})} | custom-call | flops 4294967296 | bytes 2097152 | tf_op jit(solution)/shard_map/correlate/pallas_call | solution.py:285
  115.7 3.3 %correlate.5 = bf16[2,4,512,1024]{3,2,1,0:T(8,128)(2,1)} custom-call(s32[3]{0:T(128)S(1)} %pad_add_fusion.place_ref, bf16[32,4,2,16,128]{4,3,2,1,0:T(8,128)(2,1)S(1)} %all-to-all-done.refs_0_.refs_1_, bf16[32,4,2,16,128]{4,3,2,1,0:T(8,128)(2,1)S(1)} %all-to-all-done.refs_0_.refs_1_, ...), custom_call_target="tpu_custom_call", output_to_operand_aliasing={{}: (3, {})} | custom-call | flops 4294967296 | bytes 2097152 | tf_op jit(solution)/shard_map/correlate/pallas_call | solution.py:285
  (32 shorter events, 1.4 us)
Async XLA Ops:
  1.0 6.2 %collective-permute-start = (bf16[8,4,2048]{2,1,0:T(4,128)(2,1)S(1)}, bf16[8,4,2048]{2,1,0:T(4,128)(2,1)S(1)}, u32[]{:S(2)}, u32[]{:S(2)}) collective-permute-start(bf16[8,4,2048]{2,1,0:T(4,128)(2,1)S(1)} %slice.9), channel_id=1, source_target_pairs={{0,1},{2,3},{4,5},{6,7},{8,9},{10,11},{12,13},{14,15},{16,17},{18,... | collective-permute-start | bytes 393224 | tf_op jit(solution)/shard_map/ppermute | solution.py:22
  6.1 2.2 %copy-start.2 = (bf16[8,128,2048]{2,1,0:T(8,128)(2,1)S(1)}, bf16[8,128,2048]{2,1,0:T(8,128)(2,1)}, u32[]{:S(2)}) copy-start(bf16[8,128,2048]{2,1,0:T(8,128)(2,1)} %source_ref.1) | copy-start | bytes 12582916
  6.1 2.2 %copy-start.3 = (f32[4,2048]{1,0:T(4,128)S(1)}, f32[4,2048]{1,0:T(4,128)}, u32[]{:S(2)}) copy-start(f32[4,2048]{1,0:T(4,128)} %taps_ref.1) | copy-start | bytes 98308
  12.0 2.9 %copy-start = (bf16[1024,1024]{1,0:T(8,128)(2,1)}, bf16[1024,1024]{1,0:T(8,128)(2,1)S(1)}, u32[]{:S(2)}) copy-start(bf16[1024,1024]{1,0:T(8,128)(2,1)S(1)} %get-tuple-element.22.filt_ref) | copy-start | bytes 6291460
  13.1 3.2 %collective-permute-start.7 = (bf16[64,16,128]{2,1,0:T(8,128)(2,1)S(1)}, bf16[64,16,128]{2,1,0:T(8,128)(2,1)S(1)}, u32[]{:S(2)}, u32[]{:S(2)}) collective-permute-start(bf16[64,16,128]{2,1,0:T(8,128)(2,1)S(1)} %get-tuple-element.34), channel_id=1, source_target_pairs={{0,2},{2,0},{1,3},{3,1},{4,6},{6,4},{5,7},{7,5},{8,10},{10,8},{9,1... | collective-permute-start | bytes 786440 | tf_op jit(solution)/shard_map/ppermute | solution.py:27
  14.3 2.0 %collective-permute-start.6 = (bf16[64,16,128]{2,1,0:T(8,128)(2,1)S(1)}, bf16[64,16,128]{2,1,0:T(8,128)(2,1)S(1)}, u32[]{:S(2)}, u32[]{:S(2)}) collective-permute-start(bf16[64,16,128]{2,1,0:T(8,128)(2,1)S(1)} %get-tuple-element.33), channel_id=1, source_target_pairs={{0,2},{2,0},{1,3},{3,1},{4,6},{6,4},{5,7},{7,5},{8,10},{10,8},{9,1... | collective-permute-start | bytes 786440 | tf_op jit(solution)/shard_map/ppermute | solution.py:27
  16.1 1.9 %collective-permute-start.5 = (bf16[64,16,128]{2,1,0:T(8,128)(2,1)S(1)}, bf16[64,16,128]{2,1,0:T(8,128)(2,1)S(1)}, u32[]{:S(2)}, u32[]{:S(2)}) collective-permute-start(bf16[64,16,128]{2,1,0:T(8,128)(2,1)S(1)} %get-tuple-element.28), channel_id=1, source_target_pairs={{0,2},{2,0},{1,3},{3,1},{4,6},{6,4},{5,7},{7,5},{8,10},{10,8},{9,1... | collective-permute-start | bytes 786440 | tf_op jit(solution)/shard_map/ppermute | solution.py:27
  19.6 56.1 %all-to-all-start.1 = ((bf16[64,6,16,128]{3,2,1,0:T(8,128)(2,1)}), bf16[64,6,16,128]{3,2,1,0:T(8,128)(2,1)S(1)}, u32[]{:S(2)}, u32[]{:S(2)}) async-start(bf16[64,6,16,128]{3,2,1,0:T(8,128)(2,1)} %merge.3), calls=%async_computation.1 | async-start | bytes 3145728 | tf_op jit(solution)/shard_map/all_to_all | solution.py:328
  33.5 1.6 %copy-start.1 = (bf16[1024,1024]{1,0:T(8,128)(2,1)S(1)}, bf16[1024,1024]{1,0:T(8,128)(2,1)}, u32[]{:S(2)}) copy-start(bf16[1024,1024]{1,0:T(8,128)(2,1)} %copy-done) | copy-start | bytes 6291460
  36.4 1.6 %collective-permute-start.1 = (bf16[64,16,128]{2,1,0:T(8,128)(2,1)S(1)}, bf16[64,16,128]{2,1,0:T(8,128)(2,1)S(1)}, u32[]{:S(2)}, u32[]{:S(2)}) collective-permute-start(bf16[64,16,128]{2,1,0:T(8,128)(2,1)S(1)} %get-tuple-element.24), channel_id=1, source_target_pairs={{0,2},{2,0},{1,3},{3,1},{4,6},{6,4},{5,7},{7,5},{8,10},{10,8},{9,1... | collective-permute-start | bytes 786440 | tf_op jit(solution)/shard_map/ppermute | solution.py:27
  38.6 12.3 %collective-permute-start.3 = (bf16[32,2,16,128]{3,2,1,0:T(8,128)(2,1)S(1)}, bf16[32,2,16,128]{3,2,1,0:T(8,128)(2,1)S(1)}, u32[]{:S(2)}, u32[]{:S(2)}) collective-permute-start(bf16[32,2,16,128]{3,2,1,0:T(8,128)(2,1)S(1)} %get-tuple-element.26), channel_id=1, source_target_pairs={{0,129},{1,128},{128,1},{129,0},{2,131},{3,130},{130,3},{131,2},{4... | collective-permute-start | bytes 786440 | tf_op jit(solution)/shard_map/ppermute | solution.py:27
  41.9 35.9 %collective-permute-start.2 = (bf16[32,2,16,128]{3,2,1,0:T(8,128)(2,1)S(1)}, bf16[32,2,16,128]{3,2,1,0:T(8,128)(2,1)S(1)}, u32[]{:S(2)}, u32[]{:S(2)}) collective-permute-start(bf16[32,2,16,128]{3,2,1,0:T(8,128)(2,1)S(1)} %get-tuple-element.25), channel_id=1, source_target_pairs={{0,1},{1,0},{2,3},{3,2},{4,5},{5,4},{6,7},{7,6},{8,9},{9,8},{10,11... | collective-permute-start | bytes 786440 | tf_op jit(solution)/shard_map/ppermute | solution.py:27
  50.9 26.9 %collective-permute-start.4 = (bf16[32,2,16,128]{3,2,1,0:T(8,128)(2,1)S(1)}, bf16[32,2,16,128]{3,2,1,0:T(8,128)(2,1)S(1)}, u32[]{:S(2)}, u32[]{:S(2)}) collective-permute-start(bf16[32,2,16,128]{3,2,1,0:T(8,128)(2,1)S(1)} %collective-permute-done.3), channel_id=1, source_target_pairs={{0,1},{1,0},{2,3},{3,2},{4,5},{5,4},{6,7},{7,6},{8,9},{9,8},{10,11... | collective-permute-start | bytes 786440 | tf_op jit(solution)/shard_map/ppermute | solution.py:27
  77.0 26.4 %collective-permute-start.9 = (bf16[64,4,16,128]{3,2,1,0:T(8,128)(2,1)}, bf16[64,4,16,128]{3,2,1,0:T(8,128)(2,1)}, u32[]{:S(2)}, u32[]{:S(2)}) collective-permute-start(bf16[64,4,16,128]{3,2,1,0:T(8,128)(2,1)} %slice.13), channel_id=1, source_target_pairs={{0,1},{1,0},{2,3},{3,2},{4,5},{5,4},{6,7},{7,6},{8,9},{9,8},{10,11... | collective-permute-start | bytes 3145736 | tf_op jit(solution)/shard_map/ppermute | solution.py:27
  79.0 36.7 %all-to-all-start = ((bf16[32,4,2,16,128]{4,3,2,1,0:T(8,128)(2,1)}), bf16[32,4,2,16,128]{4,3,2,1,0:T(8,128)(2,1)S(1)}, u32[]{:S(2)}, u32[]{:S(2)}) async-start(bf16[32,4,2,16,128]{4,3,2,1,0:T(8,128)(2,1)} %pad_maximum_fusion), calls=%async_computation | async-start | bytes 2097152 | tf_op jit(solution)/shard_map/all_to_all | solution.py:337
  84.7 27.7 %collective-permute-start.8 = (bf16[64,2,16,128]{3,2,1,0:T(8,128)(2,1)S(1)}, bf16[64,2,16,128]{3,2,1,0:T(8,128)(2,1)S(1)}, u32[]{:S(2)}, u32[]{:S(2)}) collective-permute-start(bf16[64,2,16,128]{3,2,1,0:T(8,128)(2,1)S(1)} %slice.12), channel_id=1, source_target_pairs={{0,1},{1,0},{2,3},{3,2},{4,5},{5,4},{6,7},{7,6},{8,9},{9,8},{10,11... | collective-permute-start | bytes 1572872 | tf_op jit(solution)/shard_map/ppermute | solution.py:27
